TPU v7x, 32 devices: a whole 2x2x4 slice. The times are simulated.
32 devices in a mesh: sub: 2 (over core), row: 4 (over y, x), col: 4 (over z).
Axes of the slice: x: 2, y: 2, z: 4, core: 2. Of those that a mesh axis runs over, the one named last changes fastest.
Arguments:
- front_entries: bfloat16 [5, 2, 4, 128, 10, 4, 128], P(None, 'sub', 'row', None, None, 'col'), may hold values from -6 to 6
- block_pattern: int32 [5, 2, 4, 10, 4], P(None, 'sub', 'row', None, 'col'), may hold values 0 or 1
- child_update: bfloat16 [2, 6, 4, 128, 6, 4, 128], P('sub', None, 'row', None, None, 'col'), may hold values from -6 to 6
- child_map: int32 [2, 6, 4], replicated, may hold values from 0 to 9, as said below
- diag_inverse: bfloat16 [1024, 1024], P('col'), may hold values from -0.0390625 to 0.0390625
Outputs:
- trailing: bfloat16 [5, 2, 4, 128, 10, 4, 128], P(None, 'sub', 'row', None, None, 'col')
Inputs may be any that keep to these rules, and one draw needn't show every extreme that they name: For each child s and each r, the 6 values child_map[s, :, r] are distinct; exactly 3 of them are even and 3 odd.
All inputs are finite; a program needn't handle non-finite values. No bound on the sum of `block_pattern` on one device may be relied on, other than what follows from the above.
Results may differ from a plain program's by a relative error of at most 0.0057.
Values may be sent and summed in bfloat16 or wider, within the bound.
No kernel may reach another device: no remote copies, remote signals or barrier semaphores. Data moves between devices by JAX's collectives and lax.ppermute only.
A program may use at most 64 MiB of HBM per device.

v0:
```python
import functools

import jax
import jax.numpy as jnp
from jax import lax
from jax.experimental import pallas as pl
from jax.experimental.pallas import tpu as pltpu
from jax.sharding import PartitionSpec as P

PANEL = 1024
ROW_TILE = 16
VMEM_BYTES = 12 * 1024 * 1024
CONTRACT = (((1,), (1,)), ((), ()))
ON_CHIP = pl.BlockSpec(memory_space=pltpu.VMEM)
SCALARS = pl.BlockSpec(memory_space=pltpu.SMEM)


def call(kernel, out_shape, in_specs, flops=0, moved=1 << 19, **more):
    single = not isinstance(out_shape, (list, tuple))
    return pl.pallas_call(
        kernel,
        out_shape=out_shape,
        in_specs=in_specs,
        out_specs=more.pop("out_specs", ON_CHIP if single else [ON_CHIP] * len(out_shape)),
        compiler_params=pltpu.CompilerParams(vmem_limit_bytes=VMEM_BYTES),
        cost_estimate=pl.CostEstimate(flops=flops, bytes_accessed=moved, transcendentals=0),
        **more,
    )


def bf16(*shape):
    return jax.ShapeDtypeStruct(shape, jnp.bfloat16)


def f32(*shape):
    return jax.ShapeDtypeStruct(shape, jnp.float32)


def flipped(block, axis, mask):
    count = lax.axis_size(axis)
    return lax.ppermute(block, axis, [(i, i ^ mask) for i in range(count)])


def shifted(block, axis, apart):
    count = lax.axis_size(axis)
    return lax.ppermute(block, axis, [(i, (i + apart) % count) for i in range(count)])


def far_last(count):
    return sorted(range(1, count), key=lambda apart: (min(apart, count - apart), apart))


def swap_even(i, count):
    return i ^ 1 if i ^ 1 < count else i


def swap_odd(i, count):
    j = ((i + 1) ^ 1) - 1
    return j if 0 <= j < count else i


@functools.cache
def line_plan(count):
    even = [swap_even(i, count) for i in range(count)]
    odd = [swap_odd(i, count) for i in range(count)]
    if count == 4:
        levels = [[(1, 0, even), (2, 0, odd)], [(3, 2, [2, 0, 3, 1]), (4, 1, [1, 3, 0, 2])]]
    else:
        levels, last = [], [0, 0]
        for step in range(count - 1):
            level = []
            for stream in (0, 1):
                level.append((1 + 2 * step + stream, last[stream], odd if (step + stream) % 2 else even))
                last[stream] = level[-1][0]
            levels.append(level)
    whose = {0: list(range(count))}
    seen = [[(0, i)] for i in range(count)]
    for level in levels:
        for array, source, to in level:
            whose[array] = [None] * count
            for i in range(count):
                whose[array][to[i]] = whose[source][i]
            for i in range(count):
                if all(whose[array][i] != origin for _, origin in seen[i]):
                    seen[i].append((array, whose[array][i]))
    origins = [[seen[i][j][1] for i in range(count)] for j in range(count)]
    places = [[seen[i][j][0] for i in range(count)] for j in range(count)]
    return levels, origins, places


class Line:
    def __init__(self, block, axis):
        self.axis = axis
        self.levels, _, self.places = line_plan(lax.axis_size(axis))
        self.held = {0: block}
        self.at = 0

    def step(self):
        for array, source, to in self.levels[self.at]:
            self.held[array] = lax.ppermute(self.held[source], self.axis, list(enumerate(to)))
        self.at += 1
        return self.at < len(self.levels)

    def fenced(self, *values):
        last = [array for array, _, _ in self.levels[self.at - 1]]
        out = fence(*values, *(self.held[array] for array in last))
        self.held.update(zip(last, out[len(values):]))
        return out[: len(values)]

    def taken(self):
        kinds = sorted({kind for row in self.places for kind in row})
        return kinds, [self.held[kind] for kind in kinds]


def among(index, members):
    found = index == members[0]
    for member in members[1:]:
        found = jnp.logical_or(found, index == member)
    return found


def looked_up(index, table):
    value = jnp.int32(table[0])
    for i, entry in enumerate(table[1:], 1):
        value = jnp.where(index == i, jnp.int32(entry), value)
    return value


def fence_kernel(*refs):
    pass


def fence(*values):
    place = pl.BlockSpec(memory_space=pl.ANY)
    return pl.pallas_call(
        fence_kernel,
        out_shape=[jax.ShapeDtypeStruct(v.shape, v.dtype) for v in values],
        in_specs=[place] * len(values),
        out_specs=[place] * len(values),
        input_output_aliases={n: n for n in range(len(values))},
        compiler_params=pltpu.CompilerParams(vmem_limit_bytes=1 << 20),
    )(*values)


def found_at(map_ref, child, place, wanted, child_count):
    at = jnp.int32(0)
    found = jnp.float32(0)
    for k in range(child_count):
        same = map_ref[child, place, k] == wanted
        at = jnp.where(same, jnp.int32(k), at)
        found = jnp.where(same, jnp.float32(1), found)
    return at, found


def block_places(map_ref, child, columns, slot_count, child_count):
    sub_index, row_index, col_index = (lax.axis_index(name) for name in ("sub", "row", "col"))
    rows = [
        found_at(map_ref, child, row_index, 2 * a + sub_index, child_count) for a in range(slot_count)
    ]
    cols = [found_at(map_ref, child, col_index, b, child_count) for b in columns]
    return rows, cols


def child_block(ref, row, col):
    return ref[row[0], col[0]].astype(jnp.float32) * (row[1] * col[1])


def line_tiles(count, share, lanes):
    return [(col, tile) for col in range(count) for tile in range(-(-(col + 1) * share // lanes))]


def pack_line(share_refs, out_ref, first, tiles):
    col_index = lax.axis_index("col")
    count = len(share_refs)
    rows, lanes = share_refs[0].shape[0], out_ref.shape[1]
    for apart, ref in zip([0, *far_last(count)], share_refs):
        for col in range(count):

            @pl.when(lax.rem(col_index + count - apart, count) == col)
            def _():
                for n, (home, tile) in enumerate(tiles):
                    if home == col:
                        out_ref[pl.ds(first + n * rows, rows), :] = ref[:, tile * lanes:(tile + 1) * lanes]


def pack_kernel(part, tiles, *refs):
    part_ref, *share_refs, out_ref = refs
    out_ref[pl.ds(0, part), :] = part_ref[...]
    pack_line(share_refs, out_ref, part, tiles)


def panel_kernel(part, groups, map_ref, pattern_ref, entries_ref, own_ref, received_ref, piece_ref, *part_refs):
    slot_count, _, size, _ = entries_ref.shape
    child_count = own_ref.shape[0]
    sub_index, row_index = lax.axis_index("sub"), lax.axis_index("row")
    places = [
        block_places(map_ref, child, range(groups), slot_count, child_count)
        for child in (sub_index, 1 - sub_index)
    ]
    for a in range(slot_count):
        for b in range(groups):
            total = entries_ref[a, b].astype(jnp.float32) * pattern_ref[a, 0, b].astype(jnp.float32)
            for (rows, cols), ref in zip(places, (own_ref, received_ref)):
                total = total + child_block(ref, rows[a], cols[b])
            piece_ref[pl.ds(a * size, size), pl.ds(b * size, size)] = total.astype(jnp.bfloat16)
    used = slot_count * size
    if used < piece_ref.shape[0]:
        piece_ref[pl.ds(used, piece_ref.shape[0] - used), :] = jnp.zeros(
            (piece_ref.shape[0] - used, piece_ref.shape[1]), piece_ref.dtype
        )
    for mask, ref in enumerate(part_refs):
        ref[...] = piece_ref[pl.ds(pl.multiple_of((row_index ^ mask) * part, ROW_TILE), part), :]


def front_kernel(groups, map_ref, pattern_ref, entries_ref, own_ref, received_ref, piece_ref, out_ref):
    slot_count, column_count, size, _ = entries_ref.shape
    child_count = own_ref.shape[0]
    sub_index = lax.axis_index("sub")
    columns = range(groups, column_count)
    places = [
        block_places(map_ref, child, columns, slot_count, child_count)
        for child in (sub_index, 1 - sub_index)
    ]
    for a in range(slot_count):
        for b in range(groups):
            out_ref[a, b] = piece_ref[pl.ds(a * size, size), pl.ds(b * size, size)]
        for n, b in enumerate(columns):
            total = entries_ref[a, b].astype(jnp.float32) * pattern_ref[a, 0, b].astype(jnp.float32)
            for (rows, cols), ref in zip(places, (own_ref, received_ref)):
                total = total + child_block(ref, rows[a], cols[n])
            out_ref[a, b] = total.astype(jnp.bfloat16)


def inverse_kernel(rows, tiles, *refs):
    *in_refs, turned_ref, out_ref = refs
    sub_index, row_index = lax.axis_index("sub"), lax.axis_index("row")
    sub_size, row_size, col_size = (lax.axis_size(name) for name in ("sub", "row", "col"))
    width = out_ref.shape[0]
    lanes = in_refs[0].shape[1]
    share = width // col_size
    lines = [
        (ref, line * len(tiles) * rows) for ref in in_refs for line in range(row_size)
    ]
    for n, (ref, first) in enumerate(lines):
        sub_at = sub_index if n < row_size else 1 - sub_index
        inside = (sub_at * row_size + (row_index ^ (n % row_size))) * rows
        for m, (col, tile) in enumerate(tiles):
            top = pl.multiple_of(col * share + inside, ROW_TILE)
            block = ref[pl.ds(first + m * rows, rows), :]
            if (tile + 1) * lanes > col * share:
                row_at = top + lax.broadcasted_iota(jnp.int32, block.shape, 0)
                col_at = tile * lanes + lax.broadcasted_iota(jnp.int32, block.shape, 1)
                block = jnp.where(col_at <= row_at, block.astype(jnp.float32), 0.0).astype(jnp.bfloat16)
            out_ref[pl.ds(top, rows), pl.ds(tile * lanes, lanes)] = block
    for col in range(col_size):
        for tile in range(width // lanes):
            if (col, tile) not in tiles:
                out_ref[pl.ds(col * share, share), pl.ds(tile * lanes, lanes)] = jnp.zeros(
                    (share, lanes), out_ref.dtype
                )
    turn_over(out_ref, turned_ref)


def turn_over(in_ref, out_ref, tile=256):
    for top in range(0, in_ref.shape[0], tile):
        for left in range(0, in_ref.shape[1], tile):
            out_ref[pl.ds(left, tile), pl.ds(top, tile)] = in_ref[pl.ds(top, tile), pl.ds(left, tile)].T


def lower_kernel(in_ref, turned_ref, out_ref):
    row_at = lax.broadcasted_iota(jnp.int32, in_ref.shape, 0)
    col_at = lax.broadcasted_iota(jnp.int32, in_ref.shape, 1)
    out_ref[...] = jnp.where(col_at <= row_at, in_ref[...].astype(jnp.float32), 0.0).astype(jnp.bfloat16)
    turn_over(out_ref, turned_ref)


def join_kernel(*refs):
    *in_refs, out_ref = refs
    rows = in_refs[0].shape[0]
    for n, ref in enumerate(in_refs):
        out_ref[pl.ds(n * rows, rows), :] = ref[...]


def joined(blocks):
    rows, width = blocks[0].shape
    return call(join_kernel, bf16(rows * len(blocks), width), [ON_CHIP] * len(blocks))(*blocks)


def inverse_shares(diag_inverse):
    part = diag_inverse.shape[0] // (lax.axis_size("sub") * lax.axis_size("row"))
    if part % ROW_TILE:
        return []
    first = (lax.axis_index("sub") * lax.axis_size("row") + lax.axis_index("row")) * part
    mine = lax.dynamic_slice_in_dim(diag_inverse, first, part, 0)
    return [mine] + [shifted(mine, "col", apart) for apart in far_last(lax.axis_size("col"))]


def turn_kernel(part, *refs):
    row_size, count = lax.axis_size("row"), lax.axis_size("col")
    held, refs = refs[:row_size], refs[row_size:]
    if len(refs) > count:
        sent_ref, *outs, lines_ref = refs
        rows = sent_ref.shape[0] - part
        lines_ref[pl.ds(0, rows), :] = sent_ref[pl.ds(part, rows), :]
        lines_ref[pl.ds(rows, rows), :] = held[1][pl.ds(part, rows), :]
    else:
        outs = refs
    row_index, col_index = lax.axis_index("row"), lax.axis_index("col")
    for apart, out_ref in enumerate(outs):
        wanted = row_index ^ lax.rem(col_index + apart, count)
        for mask, ref in enumerate(held):

            @pl.when(wanted == mask)
            def _():
                out_ref[...] = ref[pl.ds(0, part), :]


def place_piece(panel_ref, rows, block, origin, count, size):
    for g in range(block.shape[1] // size):
        left = (g * count + origin) * size
        if not isinstance(origin, int):
            left = pl.multiple_of(left, size)
        panel_ref[rows, pl.ds(left, size)] = block[:, g * size:(g + 1) * size]


def factor_from(panel_ref, inverse_ref, out_ref, tile):
    rows, width = out_ref.shape
    for first in range(0, width, tile):
        out_ref[:, pl.ds(first, tile)] = lax.dot_general(
            panel_ref[pl.ds(0, rows), pl.ds(0, first + tile)],
            inverse_ref[pl.ds(0, first + tile), pl.ds(first, tile)],
            (((1,), (0,)), ((), ())),
            preferred_element_type=jnp.float32,
        ).astype(jnp.bfloat16)


def row_factor_kernel(places, origins, kinds, size, tile, inverse_ref, *refs):
    arrays, out_ref, panel_ref = refs[: len(kinds)], refs[-2], refs[-1]
    col_index = lax.axis_index("col")
    count = len(origins)
    rows = out_ref.shape[0]
    for slot in range(count):
        origin = looked_up(col_index, origins[slot])
        for kind, ref in zip(kinds, arrays):
            members = tuple(i for i in range(count) if places[slot][i] == kind)
            if members:

                @pl.when(among(col_index, members))
                def _():
                    for top in range(0, rows, size):
                        at = pl.ds(top, size)
                        place_piece(panel_ref, at, ref[at, :], origin, count, size)

    factor_from(panel_ref, inverse_ref, out_ref, tile)


def column_factor_kernel(size, tile, inverse_ref, *refs):
    parts, out_ref, panel_ref = refs[:-2], refs[-2], refs[-1]
    row_index, col_index = lax.axis_index("row"), lax.axis_index("col")
    count = lax.axis_size("col")
    part = parts[0].shape[0] // count
    for mask, ref in enumerate(parts):
        at = pl.ds(pl.multiple_of((row_index ^ mask) * part, ROW_TILE), part)
        for apart in range(count):
            origin = lax.rem(col_index + count - apart, count)
            place_piece(panel_ref, at, ref[pl.ds(apart * part, part), :], origin, count, size)
    factor_from(panel_ref, inverse_ref, out_ref, tile)


def product_kernel(mine, step, rows_ref, columns_ref, front_ref, *refs):
    out_hbm, out_ref, sems = refs[-3:]
    sub_index = lax.axis_index("sub")
    half = sub_index if mine else 1 - sub_index
    slot_count, _, size, _ = out_ref.shape
    copies = []
    for first in range(0, slot_count, step):
        blocks = min(step, slot_count - first)
        product = lax.dot_general(
            rows_ref[pl.ds(first * size, blocks * size), :], columns_ref[...], CONTRACT,
            preferred_element_type=jnp.float32,
        )
        for m in range(first, first + blocks):
            for a in range(slot_count):
                block = product[(m - first) * size:(m - first + 1) * size, a * size:(a + 1) * size]
                out_ref[m, a] = (front_ref[m, a, half].astype(jnp.float32) - block).astype(jnp.bfloat16)
            copies.append(pltpu.make_async_copy(out_ref.at[m], out_hbm.at[m, :, half], sems.at[m]))
            copies[-1].start()
    for copy in copies:
        copy.wait()


def body(front_entries, block_pattern, child_update, child_map, diag_inverse):
    slot_count = front_entries.shape[0]
    size = front_entries.shape[3]
    column_count = front_entries.shape[4]
    child_count = child_update.shape[1]
    row_size = lax.axis_size("row")
    col_size = lax.axis_size("col")
    groups = -(-(PANEL // size) // col_size)
    tile = PANEL // 2
    rows = slot_count * size
    part = -(-rows // (row_size * ROW_TILE)) * ROW_TILE
    padded = part * row_size
    depth = groups * col_size * size
    in_hbm = pl.BlockSpec(memory_space=pltpu.HBM)
    entries = front_entries.reshape(slot_count, size, column_count, size).transpose(0, 2, 1, 3)
    pattern = block_pattern.reshape(slot_count, 1, column_count)
    slots = child_map.transpose(0, 2, 1)
    own = child_update.reshape(child_count, size, child_count, size).transpose(0, 2, 1, 3)

    received = flipped(own, "sub", 1)
    shares = inverse_shares(diag_inverse)
    lanes = groups * size
    tiles = line_tiles(col_size, diag_inverse.shape[0], lanes) if shares else []
    line_rows = len(tiles) * shares[0].shape[0] if shares else 0
    piece, *parts = call(
        functools.partial(panel_kernel, part, groups),
        [bf16(padded, lanes)] + [bf16(part, lanes)] * row_size,
        [SCALARS, SCALARS] + [ON_CHIP] * 3,
    )(slots, pattern, entries[:, :groups], own, received)
    if shares:
        parts[1] = call(
            functools.partial(pack_kernel, part, tiles), bf16(part + line_rows, lanes), [ON_CHIP] * (1 + len(shares))
        )(parts[1], *shares)
        piece, *parts = fence(piece, *parts)

    _, origins, places = line_plan(col_size)
    pieces = Line(piece, "col")
    pieces.step()
    held = [parts[0]] + [flipped(parts[mask], "row", mask) for mask in range(1, row_size)]
    sent = parts[1:2] if shares else []
    turned = call(
        functools.partial(turn_kernel, part),
        [bf16(part, lanes)] * col_size + [bf16(2 * line_rows, lanes)] * len(sent),
        [ON_CHIP] * (row_size + len(sent)),
    )(*held, *sent)
    pieces.held[1], *turned = fence(pieces.held[1], *turned)
    near, sends, lines = turned[0], turned[1:col_size], list(turned[col_size:])
    if shares:
        for bit in range(1, row_size.bit_length() - 1):
            lines += [flipped(line, "row", 1 << bit) for line in lines]
    come = {apart: shifted(sends[apart - 1], "col", apart) for apart in reversed(far_last(col_size))}
    first = far_last(col_size)[-1]
    (come[first],) = pieces.fenced(come[first])
    turned = joined([near] + [come[apart] for apart in range(1, col_size)])
    if shares:
        lines = [joined(lines)]
    turned, *lines = fence(turned, *lines)
    if shares:
        lines += [flipped(line, "sub", 1) for line in lines]
        inverse = call(
            functools.partial(inverse_kernel, shares[0].shape[0], tiles),
            bf16(PANEL, PANEL), [ON_CHIP] * len(lines), moved=4 << 20,
            scratch_shapes=[pltpu.VMEM((PANEL, PANEL), jnp.bfloat16)],
        )(*lines)
    else:
        whole = lax.all_gather(diag_inverse, "col", axis=0, tiled=True)
        inverse = call(
            lower_kernel, bf16(PANEL, PANEL), [ON_CHIP], moved=4 << 20,
            scratch_shapes=[pltpu.VMEM((PANEL, PANEL), jnp.bfloat16)],
        )(whole)
    parts = [turned] + [flipped(turned, "row", mask) for mask in range(1, row_size)]
    while pieces.at < len(pieces.levels):
        pieces.step()
    front = call(
        functools.partial(front_kernel, groups),
        bf16(slot_count, column_count, size, size),
        [SCALARS, SCALARS] + [ON_CHIP] * 4,
        moved=6 << 20,
    )(slots, pattern, entries, own, received, piece)
    kinds, arrays = pieces.taken()
    scratch = [pltpu.VMEM((padded, depth), jnp.bfloat16)]
    flops = 2 * rows * PANEL * PANEL * 3 // 4
    row_factor = call(
        functools.partial(row_factor_kernel, places, origins, kinds, size, tile),
        bf16(rows, PANEL), [ON_CHIP] * (1 + len(arrays)), flops=flops, scratch_shapes=scratch,
    )(inverse, *arrays)
    row_factor, front, inverse, *parts = fence(row_factor, front, inverse, *parts)
    front = front.reshape(slot_count, slot_count, 2, size, size)

    column_factor = call(
        functools.partial(column_factor_kernel, size, tile),
        bf16(rows, PANEL), [ON_CHIP] * (1 + row_size), flops=flops, scratch_shapes=scratch,
    )(inverse, *parts)
    other_factor = flipped(column_factor, "sub", 1)
    product = functools.partial(
        call,
        out_shape=bf16(slot_count, slot_count, 2, size, size),
        flops=2 * rows * rows * PANEL,
        out_specs=in_hbm,
        scratch_shapes=[
            pltpu.VMEM((slot_count, slot_count, size, size), jnp.bfloat16),
            pltpu.SemaphoreType.DMA((slot_count,)),
        ],
    )
    trailing = product(functools.partial(product_kernel, True, (slot_count + 1) // 2), in_specs=[ON_CHIP] * 3)(
        row_factor, column_factor, front
    )
    trailing = product(
        functools.partial(product_kernel, False, slot_count), in_specs=[ON_CHIP] * 3 + [in_hbm],
        input_output_aliases={3: 0},
    )(row_factor, other_factor, front, trailing)
    return trailing.reshape(slot_count, column_count, size, size).transpose(0, 2, 1, 3).reshape(
        slot_count, 1, 1, size, column_count, 1, size
    )


def solution(mesh):
    return jax.shard_map(
        body,
        mesh=mesh,
        in_specs=(
            P(None, "sub", "row", None, None, "col", None),
            P(None, "sub", "row", None, "col"),
            P("sub", None, "row", None, None, "col", None),
            P(),
            P("col", None),
        ),
        out_specs=P(None, "sub", "row", None, None, "col", None),
        check_vma=False,
    )
```

profile of v0, /device:TPU:0, one launch (start us, length us, event | category | flops | bytes accessed | tf_op | source)
XLA Modules:
  0.0 60.4 jit_solution(18189432245655341306)
XLA Ops:
  0.0 0.0 copy-start
  0.0 0.5 collective-permute-start
  0.5 0.6 copy-done
  1.0 4.0 %collective-permute-start.3 = (bf16[32,1024]{1,0:T(8,128)(2,1)S(1)}, bf16[32,1024]{1,0:T(8,128)(2,1)S(1)}, u32[]{:S(2)}, u32[]{:S(2)}) collective-permute-start(bf16[32,1024]{1,0:T(8,128)(2,1)S(1)} %constant_dynamic-slice_fusion.refs_1_), channel_id=1, source_target_pairs={{0,2},{1,3},{2,0},{3,1},{4,6},{5,7},{6,4},{7,5},{8,10},{9,11},{10,... | collective-permute-start | bytes 196616 | tf_op jit(solution)/shard_map/ppermute | solution.py:46
  5.1 1.3 %collective-permute-start.2 = (bf16[32,1024]{1,0:T(8,128)(2,1)S(1)}, bf16[32,1024]{1,0:T(8,128)(2,1)S(1)}, u32[]{:S(2)}, u32[]{:S(2)}) collective-permute-start(bf16[32,1024]{1,0:T(8,128)(2,1)S(1)} %constant_dynamic-slice_fusion.refs_1_), channel_id=1, source_target_pairs={{0,3},{1,0},{2,1},{3,2},{4,7},{5,4},{6,5},{7,6},{8,11},{9,8},{10,9... | collective-permute-start | bytes 196616 | tf_op jit(solution)/shard_map/ppermute | solution.py:46
  6.4 0.7 %collective-permute-start.1 = (bf16[32,1024]{1,0:T(8,128)(2,1)S(1)}, bf16[32,1024]{1,0:T(8,128)(2,1)S(1)}, u32[]{:S(2)}, u32[]{:S(2)}) collective-permute-start(bf16[32,1024]{1,0:T(8,128)(2,1)S(1)} %constant_dynamic-slice_fusion.refs_1_), channel_id=1, source_target_pairs={{0,1},{1,2},{2,3},{3,0},{4,5},{5,6},{6,7},{7,4},{8,9},{9,10},{10,1... | collective-permute-start | bytes 196616 | tf_op jit(solution)/shard_map/ppermute | solution.py:46
  7.1 1.0 %slice.4.entries_ref = bf16[5,2,128,128]{3,2,1,0:T(8,128)(2,1)S(1)} slice(bf16[5,10,128,128]{3,2,1,0:T(8,128)(2,1)} %bitcast.19), slice={[0:5], [0:2], [0:128], [0:128]} | slice | bytes 655360 | tf_op jit(solution)/shard_map/slice | solution.py:420
  8.1 0.0 collective-permute-done.received_ref
  8.1 0.0 copy-start.1
  8.1 1.3 %copy-done.1 = bf16[1,6,1,128,6,1,128]{6,3,5,4,2,1,0:T(8,128)(2,1)S(1)} copy-done((bf16[1,6,1,128,6,1,128]{6,3,5,4,2,1,0:T(8,128)(2,1)S(1)}, bf16[1,6,1,128,6,1,128]{6,3,5,4,2,1,0:T(8,128)(2,1)}, u32[]{:S(2)}) %copy-start.1) | copy-done | bytes 1179672
  9.4 0.0 copy-start.4
  9.4 0.7 %copy-done.4 = s32[2,6,4]{1,2,0:T(4,128)S(1)} copy-done((s32[2,6,4]{1,2,0:T(4,128)S(1)}, s32[2,6,4]{1,2,0:T(4,128)}, u32[]{:S(2)}) %copy-start.4) | copy-done | bytes 216
  10.1 0.7 %copy-done.6 = s32[5,1,1,10,1]{3,4,2,1,0:T(1,128)S(1)} copy-done((s32[5,1,1,10,1]{3,4,2,1,0:T(1,128)S(1)}, s32[5,1,1,10,1]{3,4,2,1,0:T(1,128)}, u32[]{:S(2)}) %copy-start.6) | copy-done | bytes 224
  10.8 0.9 %shard_map.55 = (bf16[640,256]{1,0:T(8,128)(2,1)S(1)}, bf16[160,256]{1,0:T(8,128)(2,1)S(1)}, bf16[160,256]{1,0:T(8,128)(2,1)S(1)}, bf16[160,256]{1,0:T(8,128)(2,1)S(1)}, bf16[160,256]{1,0:T(8,128)(2,1)S(1)}) custom-call(s32[2,4,6]{2,1,0:T(4,128)S(1)} %bitcast.21, s32[5,1,10]{2,1,0:T(1,128)S(1)} %bitcast.23, bf16[5,2,128,128]{3,2,1,0:T(8,128)(2,1)S(1)} %slice.4.entries_ref, ...), custom_call_target="tpu_custom_call" | custom-call | bytes 524288 | tf_op jit(solution)/shard_map/pallas_call | solution.py:416
  11.7 0.0 collective-permute-done.3.refs_4_
  11.7 0.0 collective-permute-done.2.refs_3_
  11.7 0.8 %collective-permute-done.1.refs_2_ = bf16[32,1024]{1,0:T(8,128)(2,1)S(1)} collective-permute-done((bf16[32,1024]{1,0:T(8,128)(2,1)S(1)}, bf16[32,1024]{1,0:T(8,128)(2,1)S(1)}, u32[]{:S(2)}, u32[]{:S(2)}) %collective-permute-start.1) | collective-permute-done | bytes 65568 | tf_op jit(solution)/shard_map/ppermute | solution.py:46
  12.5 0.1 shard_map.56.refs_2_
  12.6 0.9 %collective-permute-start.4 = (bf16[640,256]{1,0:T(8,128)(2,1)S(1)}, bf16[640,256]{1,0:T(8,128)(2,1)S(1)}, u32[]{:S(2)}, u32[]{:S(2)}) collective-permute-start(bf16[640,256]{1,0:T(8,128)(2,1)S(1)} %get-tuple-element.43.refs_0_.piece_ref), channel_id=1, source_target_pairs={{0,1},{1,0},{2,3},{3,2},{4,5},{5,4},{6,7},{7,6},{8,9},{9,8},{10,11... | collective-permute-start | bytes 983048 | tf_op jit(solution)/shard_map/ppermute | solution.py:100
  13.5 1.5 %collective-permute-start.5 = (bf16[480,256]{1,0:T(8,128)(2,1)S(1)}, bf16[480,256]{1,0:T(8,128)(2,1)S(1)}, u32[]{:S(2)}, u32[]{:S(2)}) collective-permute-start(bf16[480,256]{1,0:T(8,128)(2,1)S(1)} %get-tuple-element.45.refs_4_), channel_id=1, source_target_pairs={{0,4},{4,0},{8,12},{12,8},{1,5},{5,1},{9,13},{13,9},{2,6},{6,2},{1... | collective-permute-start | bytes 737288 | tf_op jit(solution)/shard_map/ppermute | solution.py:41
  15.0 1.5 %collective-permute-start.6 = (bf16[160,256]{1,0:T(8,128)(2,1)S(1)}, bf16[160,256]{1,0:T(8,128)(2,1)S(1)}, u32[]{:S(2)}, u32[]{:S(2)}) collective-permute-start(bf16[160,256]{1,0:T(8,128)(2,1)S(1)} %get-tuple-element.46), channel_id=1, source_target_pairs={{0,8},{4,12},{8,0},{12,4},{1,9},{5,13},{9,1},{13,5},{2,10},{6,14},... | collective-permute-start | bytes 245768 | tf_op jit(solution)/shard_map/ppermute | solution.py:41
  16.5 0.5 collective-permute-start.7
  17.0 0.7 %collective-permute-start.10 = (bf16[640,256]{1,0:T(8,128)(2,1)S(1)}, bf16[640,256]{1,0:T(8,128)(2,1)S(1)}, u32[]{:S(2)}, u32[]{:S(2)}) collective-permute-start(bf16[640,256]{1,0:T(8,128)(2,1)S(1)} %get-tuple-element.43.refs_0_.piece_ref), channel_id=1, source_target_pairs={{0,0},{1,2},{2,1},{3,3},{4,4},{5,6},{6,5},{7,7},{8,8},{9,10},{10,9... | collective-permute-start | bytes 983048 | tf_op jit(solution)/shard_map/ppermute | solution.py:100
  17.7 2.5 %collective-permute-done.6.refs_2_ = bf16[160,256]{1,0:T(8,128)(2,1)S(1)} collective-permute-done((bf16[160,256]{1,0:T(8,128)(2,1)S(1)}, bf16[160,256]{1,0:T(8,128)(2,1)S(1)}, u32[]{:S(2)}, u32[]{:S(2)}) %collective-permute-start.6) | collective-permute-done | bytes 81952 | tf_op jit(solution)/shard_map/ppermute | solution.py:41
  20.2 2.6 %collective-permute-done.7.refs_3_ = bf16[160,256]{1,0:T(8,128)(2,1)S(1)} collective-permute-done((bf16[160,256]{1,0:T(8,128)(2,1)S(1)}, bf16[160,256]{1,0:T(8,128)(2,1)S(1)}, u32[]{:S(2)}, u32[]{:S(2)}) %collective-permute-start.7) | collective-permute-done | bytes 81952 | tf_op jit(solution)/shard_map/ppermute | solution.py:41
  22.8 0.0 collective-permute-done.5.refs_1_
  22.8 0.1 shard_map.58
  22.9 0.0 collective-permute-done.4.refs_0_
  22.9 0.6 collective-permute-start.12
  23.5 2.1 %collective-permute-start.9 = (bf16[160,256]{1,0:T(8,128)(2,1)S(1)}, bf16[160,256]{1,0:T(8,128)(2,1)S(1)}, u32[]{:S(2)}, u32[]{:S(2)}) collective-permute-start(bf16[160,256]{1,0:T(8,128)(2,1)S(1)} %get-tuple-element.55), channel_id=1, source_target_pairs={{0,2},{1,3},{2,0},{3,1},{4,6},{5,7},{6,4},{7,5},{8,10},{9,11},{10,... | collective-permute-start | bytes 245768 | tf_op jit(solution)/shard_map/ppermute | solution.py:46
  25.6 1.3 %collective-permute-start.8 = (bf16[160,256]{1,0:T(8,128)(2,1)S(1)}, bf16[160,256]{1,0:T(8,128)(2,1)S(1)}, u32[]{:S(2)}, u32[]{:S(2)}) collective-permute-start(bf16[160,256]{1,0:T(8,128)(2,1)S(1)} %get-tuple-element.54), channel_id=1, source_target_pairs={{0,1},{1,2},{2,3},{3,0},{4,5},{5,6},{6,7},{7,4},{8,9},{9,10},{10,1... | collective-permute-start | bytes 245768 | tf_op jit(solution)/shard_map/ppermute | solution.py:46
  26.9 2.5 %collective-permute-start.11 = (bf16[160,256]{1,0:T(8,128)(2,1)S(1)}, bf16[160,256]{1,0:T(8,128)(2,1)S(1)}, u32[]{:S(2)}, u32[]{:S(2)}) collective-permute-start(bf16[160,256]{1,0:T(8,128)(2,1)S(1)} %get-tuple-element.58), channel_id=1, source_target_pairs={{0,3},{1,0},{2,1},{3,2},{4,7},{5,4},{6,5},{7,6},{8,11},{9,8},{10,9... | collective-permute-start | bytes 245768 | tf_op jit(solution)/shard_map/ppermute | solution.py:46
  29.5 0.0 collective-permute-done.10.refs_2_
  29.5 3.5 %collective-permute-done.9.refs_0_ = bf16[160,256]{1,0:T(8,128)(2,1)S(1)} collective-permute-done((bf16[160,256]{1,0:T(8,128)(2,1)S(1)}, bf16[160,256]{1,0:T(8,128)(2,1)S(1)}, u32[]{:S(2)}, u32[]{:S(2)}) %collective-permute-start.9) | collective-permute-done | bytes 81952 | tf_op jit(solution)/shard_map/ppermute | solution.py:46
  33.0 0.0 copy-start.2
  33.0 0.0 copy-start.3
  33.0 0.0 copy-start.5
  33.0 0.0 collective-permute-done.8.refs_1_
  33.0 0.1 collective-permute-done.11.refs_3_
  33.2 0.0 collective-permute-done.12.refs_1_
  33.2 0.1 collective-permute-start.13
  33.3 1.3 %collective-permute-start.15 = (bf16[640,256]{1,0:T(8,128)(2,1)S(1)}, bf16[640,256]{1,0:T(8,128)(2,1)S(1)}, u32[]{:S(2)}, u32[]{:S(2)}) collective-permute-start(bf16[640,256]{1,0:T(8,128)(2,1)S(1)} %get-tuple-element.61.refs_1_), channel_id=1, source_target_pairs={{0,1},{1,3},{2,0},{3,2},{4,5},{5,7},{6,4},{7,6},{8,9},{9,11},{10,8... | collective-permute-start | bytes 983048 | tf_op jit(solution)/shard_map/ppermute | solution.py:100
  34.6 1.7 %collective-permute-start.14 = (bf16[640,256]{1,0:T(8,128)(2,1)S(1)}, bf16[640,256]{1,0:T(8,128)(2,1)S(1)}, u32[]{:S(2)}, u32[]{:S(2)}) collective-permute-start(bf16[640,256]{1,0:T(8,128)(2,1)S(1)} %get-tuple-element.62.refs_2_), channel_id=1, source_target_pairs={{0,2},{1,0},{2,3},{3,1},{4,6},{5,4},{6,7},{7,5},{8,10},{9,8},{10,1... | collective-permute-start | bytes 983048 | tf_op jit(solution)/shard_map/ppermute | solution.py:100
  36.3 2.4 %collective-permute-start.18 = (bf16[640,256]{1,0:T(8,128)(2,1)S(1)}, bf16[640,256]{1,0:T(8,128)(2,1)S(1)}, u32[]{:S(2)}, u32[]{:S(2)}) collective-permute-start(bf16[640,256]{1,0:T(8,128)(2,1)S(1)} %get-tuple-element.63.refs_3_), channel_id=1, source_target_pairs={{0,12},{4,8},{8,4},{12,0},{1,13},{5,9},{9,5},{13,1},{2,14},{6,10},... | collective-permute-start | bytes 983048 | tf_op jit(solution)/shard_map/ppermute | solution.py:41
  38.8 0.5 collective-permute-start.17
  39.3 0.0 collective-permute-done.13.refs_1_
  39.3 0.5 collective-permute-start.16
  39.8 0.0 copy-done.2
  39.8 0.0 copy-done.3
  39.8 0.0 copy-done.5
  39.8 0.0 copy-done.7
  39.8 1.5 %shard_map.66.refs_1_ = bf16[5,10,128,128]{3,2,1,0:T(8,128)(2,1)S(1)} custom-call(s32[2,4,6]{2,1,0:T(4,128)S(1)} %bitcast.22, s32[5,1,10]{2,1,0:T(1,128)S(1)} %bitcast.24, bf16[5,10,128,128]{3,2,1,0:T(8,128)(2,1)S(1)} %bitcast.20, bf16[6,6,128,128]{3,2,1,0:T(8,128)(2,1)S(1)} %bitcast.18, bf16[6,6,128,128]{3,2,1,0:T(8,128)(2,1)S(1)} %collective-permute-done.received_ref, ...), custom_call_target="tpu_custom_call" | custom-call | bytes 6291456 | tf_op jit(solution)/shard_map/pallas_call | solution.py:465
  41.3 0.8 %shard_map.64.inverse_ref.refs_2_ = bf16[1024,1024]{1,0:T(8,128)(2,1)S(1)} custom-call(bf16[1280,256]{1,0:T(8,128)(2,1)S(1)} %get-tuple-element.60.refs_0_, bf16[1280,256]{1,0:T(8,128)(2,1)S(1)} %collective-permute-done.13.refs_1_), custom_call_target="tpu_custom_call" | custom-call | bytes 4194304 | tf_op jit(solution)/shard_map/pallas_call | solution.py:451
  42.1 2.3 %collective-permute-done.15.refs_4_ = bf16[640,256]{1,0:T(8,128)(2,1)S(1)} collective-permute-done((bf16[640,256]{1,0:T(8,128)(2,1)S(1)}, bf16[640,256]{1,0:T(8,128)(2,1)S(1)}, u32[]{:S(2)}, u32[]{:S(2)}) %collective-permute-start.15) | collective-permute-done | bytes 327712 | tf_op jit(solution)/shard_map/ppermute | solution.py:100
  44.4 6.9 %collective-permute-done.14.refs_3_ = bf16[640,256]{1,0:T(8,128)(2,1)S(1)} collective-permute-done((bf16[640,256]{1,0:T(8,128)(2,1)S(1)}, bf16[640,256]{1,0:T(8,128)(2,1)S(1)}, u32[]{:S(2)}, u32[]{:S(2)}) %collective-permute-start.14) | collective-permute-done | bytes 327712 | tf_op jit(solution)/shard_map/ppermute | solution.py:100
  51.4 1.4 %shard_map.65.refs_0_ = bf16[640,1024]{1,0:T(8,128)(2,1)S(1)} custom-call(bf16[1024,1024]{1,0:T(8,128)(2,1)S(1)} %shard_map.64.inverse_ref.refs_2_, bf16[640,256]{1,0:T(8,128)(2,1)S(1)} %get-tuple-element.43.refs_0_.piece_ref, bf16[640,256]{1,0:T(8,128)(2,1)S(1)} %get-tuple-element.61.refs_1_, bf16[640,256]{1,0:T(8,128)(2,1)S(1)} %get-tuple-element.62.refs_2_, ...), custom_call_target="tpu_custom_call" | custom-call | flops 1006632960 | bytes 524288 | tf_op jit(solution)/shard_map/pallas_call | solution.py:474
  52.8 0.0 collective-permute-done.18.refs_6_
  52.8 0.9 %collective-permute-done.17.refs_5_ = bf16[640,256]{1,0:T(8,128)(2,1)S(1)} collective-permute-done((bf16[640,256]{1,0:T(8,128)(2,1)S(1)}, bf16[640,256]{1,0:T(8,128)(2,1)S(1)}, u32[]{:S(2)}, u32[]{:S(2)}) %collective-permute-start.17) | collective-permute-done | bytes 327712 | tf_op jit(solution)/shard_map/ppermute | solution.py:41
  53.7 0.1 collective-permute-done.16.refs_4_
  53.8 1.4 %shard_map.68.columns_ref = bf16[640,1024]{1,0:T(8,128)(2,1)S(1)} custom-call(bf16[1024,1024]{1,0:T(8,128)(2,1)S(1)} %get-tuple-element.65.inverse_ref, bf16[640,256]{1,0:T(8,128)(2,1)S(1)} %get-tuple-element.66.refs_0_, bf16[640,256]{1,0:T(8,128)(2,1)S(1)} %get-tuple-element.67.refs_1_, bf16[640,256]{1,0:T(8,128)(2,1)S(1)} %get-tuple-element.68.refs_2_, ...), custom_call_target="tpu_custom_call" | custom-call | flops 1006632960 | bytes 524288 | tf_op jit(solution)/shard_map/pallas_call | solution.py:481
  55.3 0.1 collective-permute-start.19
  55.4 2.0 %shard_map.69.refs_0_ = bf16[5,5,2,128,128]{4,3,2,1,0:T(8,128)(2,1)} custom-call(bf16[640,1024]{1,0:T(8,128)(2,1)S(1)} %get-tuple-element.64.rows_ref, bf16[640,1024]{1,0:T(8,128)(2,1)S(1)} %shard_map.68.columns_ref, bf16[5,5,2,128,128]{4,3,2,1,0:T(8,128)(2,1)S(1)} %bitcast.14), custom_call_target="tpu_custom_call" | custom-call | flops 838860800 | bytes 524288 | tf_op jit(solution)/shard_map/pallas_call | solution.py:496
  57.4 1.0 %collective-permute-done.19.columns_ref = bf16[640,1024]{1,0:T(8,128)(2,1)S(1)} collective-permute-done((bf16[640,1024]{1,0:T(8,128)(2,1)S(1)}, bf16[640,1024]{1,0:T(8,128)(2,1)S(1)}, u32[]{:S(2)}, u32[]{:S(2)}) %collective-permute-start.19) | collective-permute-done | bytes 1310752 | tf_op jit(solution)/shard_map/ppermute | solution.py:41
  58.4 2.0 %shard_map.70 = bf16[5,5,2,128,128]{4,3,2,1,0:T(8,128)(2,1)} custom-call(bf16[640,1024]{1,0:T(8,128)(2,1)S(1)} %get-tuple-element.64.rows_ref, bf16[640,1024]{1,0:T(8,128)(2,1)S(1)} %collective-permute-done.19.columns_ref, bf16[5,5,2,128,128]{4,3,2,1,0:T(8,128)(2,1)S(1)} %bitcast.15, ...), custom_call_target="tpu_custom_call", output_to_operand_aliasing={{}: (3, {})} | custom-call | flops 838860800 | bytes 524288 | tf_op jit(solution)/shard_map/pallas_call | solution.py:499
  (10 shorter events, 0.1 us)
Async XLA Ops:
  0.0 1.0 %copy-start = (bf16[256,1024]{1,0:T(8,128)(2,1)S(1)}, bf16[256,1024]{1,0:T(8,128)(2,1)}, u32[]{:S(2)}) copy-start(bf16[256,1024]{1,0:T(8,128)(2,1)} %param.9) | copy-start | bytes 1572868
  0.0 8.1 %collective-permute-start = (bf16[6,6,128,128]{3,2,1,0:T(8,128)(2,1)}, bf16[6,6,128,128]{3,2,1,0:T(8,128)(2,1)S(1)}, u32[]{:S(2)}, u32[]{:S(2)}) collective-permute-start(bf16[6,6,128,128]{3,2,1,0:T(8,128)(2,1)} %bitcast.16), channel_id=1, source_target_pairs={{0,16},{16,0},{1,17},{17,1},{2,18},{18,2},{3,19},{19,3},{4,20},{20... | collective-permute-start | bytes 3538952 | tf_op jit(solution)/shard_map/ppermute | solution.py:41
  1.0 10.7 %collective-permute-start.3 = (bf16[32,1024]{1,0:T(8,128)(2,1)S(1)}, bf16[32,1024]{1,0:T(8,128)(2,1)S(1)}, u32[]{:S(2)}, u32[]{:S(2)}) collective-permute-start(bf16[32,1024]{1,0:T(8,128)(2,1)S(1)} %constant_dynamic-slice_fusion.refs_1_), channel_id=1, source_target_pairs={{0,2},{1,3},{2,0},{3,1},{4,6},{5,7},{6,4},{7,5},{8,10},{9,11},{10,... | collective-permute-start | bytes 196616 | tf_op jit(solution)/shard_map/ppermute | solution.py:46
  5.1 6.7 %collective-permute-start.2 = (bf16[32,1024]{1,0:T(8,128)(2,1)S(1)}, bf16[32,1024]{1,0:T(8,128)(2,1)S(1)}, u32[]{:S(2)}, u32[]{:S(2)}) collective-permute-start(bf16[32,1024]{1,0:T(8,128)(2,1)S(1)} %constant_dynamic-slice_fusion.refs_1_), channel_id=1, source_target_pairs={{0,3},{1,0},{2,1},{3,2},{4,7},{5,4},{6,5},{7,6},{8,11},{9,8},{10,9... | collective-permute-start | bytes 196616 | tf_op jit(solution)/shard_map/ppermute | solution.py:46
  6.4 6.1 %collective-permute-start.1 = (bf16[32,1024]{1,0:T(8,128)(2,1)S(1)}, bf16[32,1024]{1,0:T(8,128)(2,1)S(1)}, u32[]{:S(2)}, u32[]{:S(2)}) collective-permute-start(bf16[32,1024]{1,0:T(8,128)(2,1)S(1)} %constant_dynamic-slice_fusion.refs_1_), channel_id=1, source_target_pairs={{0,1},{1,2},{2,3},{3,0},{4,5},{5,6},{6,7},{7,4},{8,9},{9,10},{10,1... | collective-permute-start | bytes 196616 | tf_op jit(solution)/shard_map/ppermute | solution.py:46
  8.1 1.3 %copy-start.1 = (bf16[1,6,1,128,6,1,128]{6,3,5,4,2,1,0:T(8,128)(2,1)S(1)}, bf16[1,6,1,128,6,1,128]{6,3,5,4,2,1,0:T(8,128)(2,1)}, u32[]{:S(2)}) copy-start(bf16[1,6,1,128,6,1,128]{6,3,5,4,2,1,0:T(8,128)(2,1)} %param.7) | copy-start | bytes 3538948
  9.4 0.7 %copy-start.4 = (s32[2,6,4]{1,2,0:T(4,128)S(1)}, s32[2,6,4]{1,2,0:T(4,128)}, u32[]{:S(2)}) copy-start(s32[2,6,4]{1,2,0:T(4,128)} %param.8) | copy-start | bytes 580
  10.1 0.7 %copy-start.6 = (s32[5,1,1,10,1]{3,4,2,1,0:T(1,128)S(1)}, s32[5,1,1,10,1]{3,4,2,1,0:T(1,128)}, u32[]{:S(2)}) copy-start(s32[5,1,1,10,1]{3,4,2,1,0:T(1,128)} %param.6) | copy-start | bytes 604
  12.6 10.3 %collective-permute-start.4 = (bf16[640,256]{1,0:T(8,128)(2,1)S(1)}, bf16[640,256]{1,0:T(8,128)(2,1)S(1)}, u32[]{:S(2)}, u32[]{:S(2)}) collective-permute-start(bf16[640,256]{1,0:T(8,128)(2,1)S(1)} %get-tuple-element.43.refs_0_.piece_ref), channel_id=1, source_target_pairs={{0,1},{1,0},{2,3},{3,2},{4,5},{5,4},{6,7},{7,6},{8,9},{9,8},{10,11... | collective-permute-start | bytes 983048 | tf_op jit(solution)/shard_map/ppermute | solution.py:100
  13.5 9.3 %collective-permute-start.5 = (bf16[480,256]{1,0:T(8,128)(2,1)S(1)}, bf16[480,256]{1,0:T(8,128)(2,1)S(1)}, u32[]{:S(2)}, u32[]{:S(2)}) collective-permute-start(bf16[480,256]{1,0:T(8,128)(2,1)S(1)} %get-tuple-element.45.refs_4_), channel_id=1, source_target_pairs={{0,4},{4,0},{8,12},{12,8},{1,5},{5,1},{9,13},{13,9},{2,6},{6,2},{1... | collective-permute-start | bytes 737288 | tf_op jit(solution)/shard_map/ppermute | solution.py:41
  15.0 5.2 %collective-permute-start.6 = (bf16[160,256]{1,0:T(8,128)(2,1)S(1)}, bf16[160,256]{1,0:T(8,128)(2,1)S(1)}, u32[]{:S(2)}, u32[]{:S(2)}) collective-permute-start(bf16[160,256]{1,0:T(8,128)(2,1)S(1)} %get-tuple-element.46), channel_id=1, source_target_pairs={{0,8},{4,12},{8,0},{12,4},{1,9},{5,13},{9,1},{13,5},{2,10},{6,14},... | collective-permute-start | bytes 245768 | tf_op jit(solution)/shard_map/ppermute | solution.py:41
  16.5 6.3 %collective-permute-start.7 = (bf16[160,256]{1,0:T(8,128)(2,1)S(1)}, bf16[160,256]{1,0:T(8,128)(2,1)S(1)}, u32[]{:S(2)}, u32[]{:S(2)}) collective-permute-start(bf16[160,256]{1,0:T(8,128)(2,1)S(1)} %get-tuple-element.47), channel_id=1, source_target_pairs={{0,12},{4,8},{8,4},{12,0},{1,13},{5,9},{9,5},{13,1},{2,14},{6,10},... | collective-permute-start | bytes 245768 | tf_op jit(solution)/shard_map/ppermute | solution.py:41
  17.0 12.5 %collective-permute-start.10 = (bf16[640,256]{1,0:T(8,128)(2,1)S(1)}, bf16[640,256]{1,0:T(8,128)(2,1)S(1)}, u32[]{:S(2)}, u32[]{:S(2)}) collective-permute-start(bf16[640,256]{1,0:T(8,128)(2,1)S(1)} %get-tuple-element.43.refs_0_.piece_ref), channel_id=1, source_target_pairs={{0,0},{1,2},{2,1},{3,3},{4,4},{5,6},{6,5},{7,7},{8,8},{9,10},{10,9... | collective-permute-start | bytes 983048 | tf_op jit(solution)/shard_map/ppermute | solution.py:100
  22.9 10.2 %collective-permute-start.12 = (bf16[640,256]{1,0:T(8,128)(2,1)S(1)}, bf16[640,256]{1,0:T(8,128)(2,1)S(1)}, u32[]{:S(2)}, u32[]{:S(2)}) collective-permute-start(bf16[640,256]{1,0:T(8,128)(2,1)S(1)} %get-tuple-element.59.refs_0_), channel_id=1, source_target_pairs={{0,8},{4,12},{8,0},{12,4},{1,9},{5,13},{9,1},{13,5},{2,10},{6,14},... | collective-permute-start | bytes 983048 | tf_op jit(solution)/shard_map/ppermute | solution.py:41
  23.5 9.5 %collective-permute-start.9 = (bf16[160,256]{1,0:T(8,128)(2,1)S(1)}, bf16[160,256]{1,0:T(8,128)(2,1)S(1)}, u32[]{:S(2)}, u32[]{:S(2)}) collective-permute-start(bf16[160,256]{1,0:T(8,128)(2,1)S(1)} %get-tuple-element.55), channel_id=1, source_target_pairs={{0,2},{1,3},{2,0},{3,1},{4,6},{5,7},{6,4},{7,5},{8,10},{9,11},{10,... | collective-permute-start | bytes 245768 | tf_op jit(solution)/shard_map/ppermute | solution.py:46
  25.6 7.3 %collective-permute-start.8 = (bf16[160,256]{1,0:T(8,128)(2,1)S(1)}, bf16[160,256]{1,0:T(8,128)(2,1)S(1)}, u32[]{:S(2)}, u32[]{:S(2)}) collective-permute-start(bf16[160,256]{1,0:T(8,128)(2,1)S(1)} %get-tuple-element.54), channel_id=1, source_target_pairs={{0,1},{1,2},{2,3},{3,0},{4,5},{5,6},{6,7},{7,4},{8,9},{9,10},{10,1... | collective-permute-start | bytes 245768 | tf_op jit(solution)/shard_map/ppermute | solution.py:46
  26.9 6.2 %collective-permute-start.11 = (bf16[160,256]{1,0:T(8,128)(2,1)S(1)}, bf16[160,256]{1,0:T(8,128)(2,1)S(1)}, u32[]{:S(2)}, u32[]{:S(2)}) collective-permute-start(bf16[160,256]{1,0:T(8,128)(2,1)S(1)} %get-tuple-element.58), channel_id=1, source_target_pairs={{0,3},{1,0},{2,1},{3,2},{4,7},{5,4},{6,5},{7,6},{8,11},{9,8},{10,9... | collective-permute-start | bytes 245768 | tf_op jit(solution)/shard_map/ppermute | solution.py:46
  33.0 6.8 %copy-start.2 = (bf16[1,6,1,128,6,1,128]{6,3,5,4,2,1,0:T(8,128)(2,1)S(1)}, bf16[1,6,1,128,6,1,128]{6,3,5,4,2,1,0:T(8,128)(2,1)}, u32[]{:S(2)}) copy-start(bf16[1,6,1,128,6,1,128]{6,3,5,4,2,1,0:T(8,128)(2,1)} %param.7) | copy-start | bytes 3538948
  33.0 6.8 %copy-start.3 = (bf16[5,1,1,128,10,1,128]{6,3,5,4,2,1,0:T(8,128)(2,1)S(1)}, bf16[5,1,1,128,10,1,128]{6,3,5,4,2,1,0:T(8,128)(2,1)}, u32[]{:S(2)}) copy-start(bf16[5,1,1,128,10,1,128]{6,3,5,4,2,1,0:T(8,128)(2,1)} %param.5) | copy-start | bytes 4915204
  33.0 6.8 %copy-start.5 = (s32[2,6,4]{1,2,0:T(4,128)S(1)}, s32[2,6,4]{1,2,0:T(4,128)}, u32[]{:S(2)}) copy-start(s32[2,6,4]{1,2,0:T(4,128)} %param.8) | copy-start | bytes 580
  33.0 6.8 %copy-start.7 = (s32[5,1,1,10,1]{3,4,2,1,0:T(1,128)S(1)}, s32[5,1,1,10,1]{3,4,2,1,0:T(1,128)}, u32[]{:S(2)}) copy-start(s32[5,1,1,10,1]{3,4,2,1,0:T(1,128)} %param.6) | copy-start | bytes 604
  33.2 6.0 %collective-permute-start.13 = (bf16[1280,256]{1,0:T(8,128)(2,1)S(1)}, bf16[1280,256]{1,0:T(8,128)(2,1)S(1)}, u32[]{:S(2)}, u32[]{:S(2)}) collective-permute-start(bf16[1280,256]{1,0:T(8,128)(2,1)S(1)} %get-tuple-element.60.refs_0_), channel_id=1, source_target_pairs={{0,16},{16,0},{1,17},{17,1},{2,18},{18,2},{3,19},{19,3},{4,20},{20... | collective-permute-start | bytes 1966088 | tf_op jit(solution)/shard_map/ppermute | solution.py:41
  33.3 11.1 %collective-permute-start.15 = (bf16[640,256]{1,0:T(8,128)(2,1)S(1)}, bf16[640,256]{1,0:T(8,128)(2,1)S(1)}, u32[]{:S(2)}, u32[]{:S(2)}) collective-permute-start(bf16[640,256]{1,0:T(8,128)(2,1)S(1)} %get-tuple-element.61.refs_1_), channel_id=1, source_target_pairs={{0,1},{1,3},{2,0},{3,2},{4,5},{5,7},{6,4},{7,6},{8,9},{9,11},{10,8... | collective-permute-start | bytes 983048 | tf_op jit(solution)/shard_map/ppermute | solution.py:100
  34.6 16.8 %collective-permute-start.14 = (bf16[640,256]{1,0:T(8,128)(2,1)S(1)}, bf16[640,256]{1,0:T(8,128)(2,1)S(1)}, u32[]{:S(2)}, u32[]{:S(2)}) collective-permute-start(bf16[640,256]{1,0:T(8,128)(2,1)S(1)} %get-tuple-element.62.refs_2_), channel_id=1, source_target_pairs={{0,2},{1,0},{2,3},{3,1},{4,6},{5,4},{6,7},{7,5},{8,10},{9,8},{10,1... | collective-permute-start | bytes 983048 | tf_op jit(solution)/shard_map/ppermute | solution.py:100
  36.3 16.5 %collective-permute-start.18 = (bf16[640,256]{1,0:T(8,128)(2,1)S(1)}, bf16[640,256]{1,0:T(8,128)(2,1)S(1)}, u32[]{:S(2)}, u32[]{:S(2)}) collective-permute-start(bf16[640,256]{1,0:T(8,128)(2,1)S(1)} %get-tuple-element.63.refs_3_), channel_id=1, source_target_pairs={{0,12},{4,8},{8,4},{12,0},{1,13},{5,9},{9,5},{13,1},{2,14},{6,10},... | collective-permute-start | bytes 983048 | tf_op jit(solution)/shard_map/ppermute | solution.py:41
  38.8 15.0 %collective-permute-start.17 = (bf16[640,256]{1,0:T(8,128)(2,1)S(1)}, bf16[640,256]{1,0:T(8,128)(2,1)S(1)}, u32[]{:S(2)}, u32[]{:S(2)}) collective-permute-start(bf16[640,256]{1,0:T(8,128)(2,1)S(1)} %get-tuple-element.63.refs_3_), channel_id=1, source_target_pairs={{0,8},{4,12},{8,0},{12,4},{1,9},{5,13},{9,1},{13,5},{2,10},{6,14},... | collective-permute-start | bytes 983048 | tf_op jit(solution)/shard_map/ppermute | solution.py:41
  39.3 14.6 %collective-permute-start.16 = (bf16[640,256]{1,0:T(8,128)(2,1)S(1)}, bf16[640,256]{1,0:T(8,128)(2,1)S(1)}, u32[]{:S(2)}, u32[]{:S(2)}) collective-permute-start(bf16[640,256]{1,0:T(8,128)(2,1)S(1)} %get-tuple-element.63.refs_3_), channel_id=1, source_target_pairs={{0,4},{4,0},{8,12},{12,8},{1,5},{5,1},{9,13},{13,9},{2,6},{6,2},{1... | collective-permute-start | bytes 983048 | tf_op jit(solution)/shard_map/ppermute | solution.py:41
  55.3 3.1 %collective-permute-start.19 = (bf16[640,1024]{1,0:T(8,128)(2,1)S(1)}, bf16[640,1024]{1,0:T(8,128)(2,1)S(1)}, u32[]{:S(2)}, u32[]{:S(2)}) collective-permute-start(bf16[640,1024]{1,0:T(8,128)(2,1)S(1)} %shard_map.68.columns_ref), channel_id=1, source_target_pairs={{0,16},{16,0},{1,17},{17,1},{2,18},{18,2},{3,19},{19,3},{4,20},{20... | collective-permute-start | bytes 3932168 | tf_op jit(solution)/shard_map/ppermute | solution.py:41
where the time goes:
time: 60.7 us; the launch traced here: 60.4 us
  starting transfers between devices  24.7 us (41%)
  waiting for transfers between devices  20.8 us (34%)
  Pallas kernels  10.4 us (17%)
  local copies, waits for them, and re-layouts  4.24 us (7%)
    ppermute x6, starting transfers between devices, shifted(): lax.ppermute(block, axis, [(i, (i + apart) % count) for i in range(count)])  12 us
    ppermute x4, waiting for transfers between devices, step(): lax.ppermute(self.held[source], self.axis, list(enumerate(to)))  9.26 us
    ppermute x10, starting transfers between devices, flipped(): return lax.ppermute(block, axis, [(i, i ^ mask) for i in range(count)])  8.14 us
    ppermute x10, waiting for transfers between devices, flipped(): return lax.ppermute(block, axis, [(i, i ^ mask) for i in range(count)])  7.15 us
    ppermute x4, starting transfers between devices, step(): lax.ppermute(self.held[source], self.axis, list(enumerate(to)))  4.55 us
    ppermute x6, waiting for transfers between devices, shifted(): lax.ppermute(block, axis, [(i, (i + apart) % count) for i in range(count)])  4.4 us
    unnamed x16, local copies, waits for them, and re-layouts  3.24 us
    pallas_call x1, Pallas kernels, body(): product(functools.partial(product_kernel, False, slot_count), in_specs=[O...  2.02 us
  transfers between devices with their start and end apart: 20, of which 10 were waited for; matrix products, arithmetic and copies ran while one was open for 2% of the time, Pallas kernels for 11%

commit v1 on v0

--- a/solution.py
+++ b/solution.py
@@ -354,37 +354,47 @@
     factor_from(panel_ref, inverse_ref, out_ref, tile)
 
 
-def column_factor_kernel(size, tile, inverse_ref, *refs):
-    parts, out_ref, panel_ref = refs[:-2], refs[-2], refs[-1]
+def column_factor_kernel(size, count, inverse_ref, *refs):
+    parts, outs, panel_ref = refs[: -1 - count], refs[-1 - count:-1], refs[-1]
     row_index, col_index = lax.axis_index("row"), lax.axis_index("col")
-    count = lax.axis_size("col")
-    part = parts[0].shape[0] // count
+    col_size = lax.axis_size("col")
+    part = parts[0].shape[0] // col_size
+    rows, tile = outs[0].shape
     for mask, ref in enumerate(parts):
         at = pl.ds(pl.multiple_of((row_index ^ mask) * part, ROW_TILE), part)
-        for apart in range(count):
-            origin = lax.rem(col_index + count - apart, count)
-            place_piece(panel_ref, at, ref[pl.ds(apart * part, part), :], origin, count, size)
-    factor_from(panel_ref, inverse_ref, out_ref, tile)
-
-
-def product_kernel(mine, step, rows_ref, columns_ref, front_ref, *refs):
+        for apart in range(col_size):
+            origin = lax.rem(col_index + col_size - apart, col_size)
+            place_piece(panel_ref, at, ref[pl.ds(apart * part, part), :], origin, col_size, size)
+    for n, out_ref in enumerate(outs):
+        first = n * tile
+        out_ref[...] = lax.dot_general(
+            panel_ref[pl.ds(0, rows), pl.ds(0, first + tile)],
+            inverse_ref[pl.ds(0, first + tile), pl.ds(first, tile)],
+            (((1,), (0,)), ((), ())),
+            preferred_element_type=jnp.float32,
+        ).astype(jnp.bfloat16)
+
+
+def product_kernel(mine, halves, rows_ref, front_ref, *refs):
+    columns_refs = refs[:halves]
     out_hbm, out_ref, sems = refs[-3:]
     sub_index = lax.axis_index("sub")
     half = sub_index if mine else 1 - sub_index
     slot_count, _, size, _ = out_ref.shape
     copies = []
-    for first in range(0, slot_count, step):
-        blocks = min(step, slot_count - first)
-        product = lax.dot_general(
-            rows_ref[pl.ds(first * size, blocks * size), :], columns_ref[...], CONTRACT,
-            preferred_element_type=jnp.float32,
+    product = None
+    for n, ref in enumerate(columns_refs):
+        width = ref.shape[1]
+        share = lax.dot_general(
+            rows_ref[:, pl.ds(n * width, width)], ref[...], CONTRACT, preferred_element_type=jnp.float32
         )
-        for m in range(first, first + blocks):
-            for a in range(slot_count):
-                block = product[(m - first) * size:(m - first + 1) * size, a * size:(a + 1) * size]
-                out_ref[m, a] = (front_ref[m, a, half].astype(jnp.float32) - block).astype(jnp.bfloat16)
-            copies.append(pltpu.make_async_copy(out_ref.at[m], out_hbm.at[m, :, half], sems.at[m]))
-            copies[-1].start()
+        product = share if product is None else product + share
+    for m in range(slot_count):
+        for a in range(slot_count):
+            block = product[m * size:(m + 1) * size, a * size:(a + 1) * size]
+            out_ref[m, a] = (front_ref[m, a, half].astype(jnp.float32) - block).astype(jnp.bfloat16)
+        copies.append(pltpu.make_async_copy(out_ref.at[m], out_hbm.at[m, :, half], sems.at[m]))
+        copies[-1].start()
     for copy in copies:
         copy.wait()
 
@@ -478,11 +488,12 @@
     row_factor, front, inverse, *parts = fence(row_factor, front, inverse, *parts)
     front = front.reshape(slot_count, slot_count, 2, size, size)
 
+    halves = PANEL // tile
     column_factor = call(
-        functools.partial(column_factor_kernel, size, tile),
-        bf16(rows, PANEL), [ON_CHIP] * (1 + row_size), flops=flops, scratch_shapes=scratch,
+        functools.partial(column_factor_kernel, size, halves),
+        [bf16(rows, tile)] * halves, [ON_CHIP] * (1 + row_size), flops=flops, scratch_shapes=scratch,
     )(inverse, *parts)
-    other_factor = flipped(column_factor, "sub", 1)
+    other_factor = [flipped(share, "sub", 1) for share in column_factor]
     product = functools.partial(
         call,
         out_shape=bf16(slot_count, slot_count, 2, size, size),
@@ -493,13 +504,13 @@
             pltpu.SemaphoreType.DMA((slot_count,)),
         ],
     )
-    trailing = product(functools.partial(product_kernel, True, (slot_count + 1) // 2), in_specs=[ON_CHIP] * 3)(
-        row_factor, column_factor, front
-    )
     trailing = product(
-        functools.partial(product_kernel, False, slot_count), in_specs=[ON_CHIP] * 3 + [in_hbm],
-        input_output_aliases={3: 0},
-    )(row_factor, other_factor, front, trailing)
+        functools.partial(product_kernel, True, halves), in_specs=[ON_CHIP] * (2 + halves)
+    )(row_factor, front, *column_factor)
+    trailing = product(
+        functools.partial(product_kernel, False, halves), in_specs=[ON_CHIP] * (2 + halves) + [in_hbm],
+        input_output_aliases={2 + halves: 0},
+    )(row_factor, front, *other_factor, trailing)
     return trailing.reshape(slot_count, column_count, size, size).transpose(0, 2, 1, 3).reshape(
         slot_count, 1, 1, size, column_count, 1, size
     )

time: 60.7 us -> 60.7 us (level)
    ppermute x10 -> x11, waiting for transfers between devices: 7.15 us -> 6.64 us  [flipped(): return lax.ppermute(block, axis, [(i, i ^ mask) for i in range(count)])]
    ppermute x10 -> x11, starting transfers between devices: 8.14 us -> 8.64 us  [flipped(): return lax.ppermute(block, axis, [(i, i ^ mask) for i in range(count)])]
  transfers between devices with their start and end apart: 20 -> 21, of which waited for: 10 -> 10; matrix products, arithmetic and copies ran while one was open for 2% -> 2% of each run, Pallas kernels for 11% -> 11%
where the time goes in v1:
time: 60.7 us; the launch traced here: 60.4 us
  starting transfers between devices  25.2 us (42%)
  waiting for transfers between devices  20.3 us (33%)
  Pallas kernels  10.4 us (17%)
  local copies, waits for them, and re-layouts  4.24 us (7%)
    ppermute x6, starting transfers between devices, shifted(): lax.ppermute(block, axis, [(i, (i + apart) % count) for i in range(count)])  12 us
    ppermute x4, waiting for transfers between devices, step(): lax.ppermute(self.held[source], self.axis, list(enumerate(to)))  9.26 us
    ppermute x11, starting transfers between devices, flipped(): return lax.ppermute(block, axis, [(i, i ^ mask) for i in range(count)])  8.64 us
    ppermute x11, waiting for transfers between devices, flipped(): return lax.ppermute(block, axis, [(i, i ^ mask) for i in range(count)])  6.64 us
    ppermute x4, starting transfers between devices, step(): lax.ppermute(self.held[source], self.axis, list(enumerate(to)))  4.55 us
    ppermute x6, waiting for transfers between devices, shifted(): lax.ppermute(block, axis, [(i, (i + apart) % count) for i in range(count)])  4.4 us
    unnamed x16, local copies, waits for them, and re-layouts  3.24 us
    pallas_call x1, Pallas kernels, body(): product(functools.partial(product_kernel, True, halves), in_specs=[ON_CHI...  2 us
  transfers between devices with their start and end apart: 21, of which 10 were waited for; matrix products, arithmetic and copies ran while one was open for 2% of the time, Pallas kernels for 11%

profile of v1, /device:TPU:0, one launch (start us, length us, event | category | flops | bytes accessed | tf_op | source)
XLA Modules:
  0.0 60.4 jit_solution(18207831917486993332)
XLA Ops:
  0.0 0.0 copy-start
  0.0 0.5 collective-permute-start
  0.5 0.6 copy-done
  1.0 4.0 %collective-permute-start.3 = (bf16[32,1024]{1,0:T(8,128)(2,1)S(1)}, bf16[32,1024]{1,0:T(8,128)(2,1)S(1)}, u32[]{:S(2)}, u32[]{:S(2)}) collective-permute-start(bf16[32,1024]{1,0:T(8,128)(2,1)S(1)} %constant_dynamic-slice_fusion.refs_1_), channel_id=1, source_target_pairs={{0,2},{1,3},{2,0},{3,1},{4,6},{5,7},{6,4},{7,5},{8,10},{9,11},{10,... | collective-permute-start | bytes 196616 | tf_op jit(solution)/shard_map/ppermute | solution.py:46
  5.1 1.3 %collective-permute-start.2 = (bf16[32,1024]{1,0:T(8,128)(2,1)S(1)}, bf16[32,1024]{1,0:T(8,128)(2,1)S(1)}, u32[]{:S(2)}, u32[]{:S(2)}) collective-permute-start(bf16[32,1024]{1,0:T(8,128)(2,1)S(1)} %constant_dynamic-slice_fusion.refs_1_), channel_id=1, source_target_pairs={{0,3},{1,0},{2,1},{3,2},{4,7},{5,4},{6,5},{7,6},{8,11},{9,8},{10,9... | collective-permute-start | bytes 196616 | tf_op jit(solution)/shard_map/ppermute | solution.py:46
  6.4 0.7 %collective-permute-start.1 = (bf16[32,1024]{1,0:T(8,128)(2,1)S(1)}, bf16[32,1024]{1,0:T(8,128)(2,1)S(1)}, u32[]{:S(2)}, u32[]{:S(2)}) collective-permute-start(bf16[32,1024]{1,0:T(8,128)(2,1)S(1)} %constant_dynamic-slice_fusion.refs_1_), channel_id=1, source_target_pairs={{0,1},{1,2},{2,3},{3,0},{4,5},{5,6},{6,7},{7,4},{8,9},{9,10},{10,1... | collective-permute-start | bytes 196616 | tf_op jit(solution)/shard_map/ppermute | solution.py:46
  7.1 1.0 %slice.4.entries_ref = bf16[5,2,128,128]{3,2,1,0:T(8,128)(2,1)S(1)} slice(bf16[5,10,128,128]{3,2,1,0:T(8,128)(2,1)} %bitcast.19), slice={[0:5], [0:2], [0:128], [0:128]} | slice | bytes 655360 | tf_op jit(solution)/shard_map/slice | solution.py:430
  8.1 0.0 collective-permute-done.received_ref
  8.1 0.0 copy-start.1
  8.1 1.3 %copy-done.1 = bf16[1,6,1,128,6,1,128]{6,3,5,4,2,1,0:T(8,128)(2,1)S(1)} copy-done((bf16[1,6,1,128,6,1,128]{6,3,5,4,2,1,0:T(8,128)(2,1)S(1)}, bf16[1,6,1,128,6,1,128]{6,3,5,4,2,1,0:T(8,128)(2,1)}, u32[]{:S(2)}) %copy-start.1) | copy-done | bytes 1179672
  9.4 0.0 copy-start.4
  9.4 0.7 %copy-done.4 = s32[2,6,4]{1,2,0:T(4,128)S(1)} copy-done((s32[2,6,4]{1,2,0:T(4,128)S(1)}, s32[2,6,4]{1,2,0:T(4,128)}, u32[]{:S(2)}) %copy-start.4) | copy-done | bytes 216
  10.1 0.7 %copy-done.6 = s32[5,1,1,10,1]{3,4,2,1,0:T(1,128)S(1)} copy-done((s32[5,1,1,10,1]{3,4,2,1,0:T(1,128)S(1)}, s32[5,1,1,10,1]{3,4,2,1,0:T(1,128)}, u32[]{:S(2)}) %copy-start.6) | copy-done | bytes 224
  10.8 0.9 %shard_map.55 = (bf16[640,256]{1,0:T(8,128)(2,1)S(1)}, bf16[160,256]{1,0:T(8,128)(2,1)S(1)}, bf16[160,256]{1,0:T(8,128)(2,1)S(1)}, bf16[160,256]{1,0:T(8,128)(2,1)S(1)}, bf16[160,256]{1,0:T(8,128)(2,1)S(1)}) custom-call(s32[2,4,6]{2,1,0:T(4,128)S(1)} %bitcast.21, s32[5,1,10]{2,1,0:T(1,128)S(1)} %bitcast.23, bf16[5,2,128,128]{3,2,1,0:T(8,128)(2,1)S(1)} %slice.4.entries_ref, ...), custom_call_target="tpu_custom_call" | custom-call | bytes 524288 | tf_op jit(solution)/shard_map/pallas_call | solution.py:426
  11.7 0.0 collective-permute-done.3.refs_4_
  11.7 0.0 collective-permute-done.2.refs_3_
  11.7 0.8 %collective-permute-done.1.refs_2_ = bf16[32,1024]{1,0:T(8,128)(2,1)S(1)} collective-permute-done((bf16[32,1024]{1,0:T(8,128)(2,1)S(1)}, bf16[32,1024]{1,0:T(8,128)(2,1)S(1)}, u32[]{:S(2)}, u32[]{:S(2)}) %collective-permute-start.1) | collective-permute-done | bytes 65568 | tf_op jit(solution)/shard_map/ppermute | solution.py:46
  12.5 0.1 shard_map.56.refs_2_
  12.6 0.9 %collective-permute-start.4 = (bf16[640,256]{1,0:T(8,128)(2,1)S(1)}, bf16[640,256]{1,0:T(8,128)(2,1)S(1)}, u32[]{:S(2)}, u32[]{:S(2)}) collective-permute-start(bf16[640,256]{1,0:T(8,128)(2,1)S(1)} %get-tuple-element.45.refs_0_.piece_ref), channel_id=1, source_target_pairs={{0,1},{1,0},{2,3},{3,2},{4,5},{5,4},{6,7},{7,6},{8,9},{9,8},{10,11... | collective-permute-start | bytes 983048 | tf_op jit(solution)/shard_map/ppermute | solution.py:100
  13.5 1.5 %collective-permute-start.5 = (bf16[480,256]{1,0:T(8,128)(2,1)S(1)}, bf16[480,256]{1,0:T(8,128)(2,1)S(1)}, u32[]{:S(2)}, u32[]{:S(2)}) collective-permute-start(bf16[480,256]{1,0:T(8,128)(2,1)S(1)} %get-tuple-element.47.refs_4_), channel_id=1, source_target_pairs={{0,4},{4,0},{8,12},{12,8},{1,5},{5,1},{9,13},{13,9},{2,6},{6,2},{1... | collective-permute-start | bytes 737288 | tf_op jit(solution)/shard_map/ppermute | solution.py:41
  15.0 1.5 %collective-permute-start.6 = (bf16[160,256]{1,0:T(8,128)(2,1)S(1)}, bf16[160,256]{1,0:T(8,128)(2,1)S(1)}, u32[]{:S(2)}, u32[]{:S(2)}) collective-permute-start(bf16[160,256]{1,0:T(8,128)(2,1)S(1)} %get-tuple-element.48), channel_id=1, source_target_pairs={{0,8},{4,12},{8,0},{12,4},{1,9},{5,13},{9,1},{13,5},{2,10},{6,14},... | collective-permute-start | bytes 245768 | tf_op jit(solution)/shard_map/ppermute | solution.py:41
  16.5 0.5 collective-permute-start.7
  17.0 0.7 %collective-permute-start.10 = (bf16[640,256]{1,0:T(8,128)(2,1)S(1)}, bf16[640,256]{1,0:T(8,128)(2,1)S(1)}, u32[]{:S(2)}, u32[]{:S(2)}) collective-permute-start(bf16[640,256]{1,0:T(8,128)(2,1)S(1)} %get-tuple-element.45.refs_0_.piece_ref), channel_id=1, source_target_pairs={{0,0},{1,2},{2,1},{3,3},{4,4},{5,6},{6,5},{7,7},{8,8},{9,10},{10,9... | collective-permute-start | bytes 983048 | tf_op jit(solution)/shard_map/ppermute | solution.py:100
  17.7 2.5 %collective-permute-done.6.refs_2_ = bf16[160,256]{1,0:T(8,128)(2,1)S(1)} collective-permute-done((bf16[160,256]{1,0:T(8,128)(2,1)S(1)}, bf16[160,256]{1,0:T(8,128)(2,1)S(1)}, u32[]{:S(2)}, u32[]{:S(2)}) %collective-permute-start.6) | collective-permute-done | bytes 81952 | tf_op jit(solution)/shard_map/ppermute | solution.py:41
  20.2 2.6 %collective-permute-done.7.refs_3_ = bf16[160,256]{1,0:T(8,128)(2,1)S(1)} collective-permute-done((bf16[160,256]{1,0:T(8,128)(2,1)S(1)}, bf16[160,256]{1,0:T(8,128)(2,1)S(1)}, u32[]{:S(2)}, u32[]{:S(2)}) %collective-permute-start.7) | collective-permute-done | bytes 81952 | tf_op jit(solution)/shard_map/ppermute | solution.py:41
  22.8 0.0 collective-permute-done.5.refs_1_
  22.8 0.1 shard_map.58
  22.9 0.0 collective-permute-done.4.refs_0_
  22.9 0.6 collective-permute-start.12
  23.5 2.1 %collective-permute-start.9 = (bf16[160,256]{1,0:T(8,128)(2,1)S(1)}, bf16[160,256]{1,0:T(8,128)(2,1)S(1)}, u32[]{:S(2)}, u32[]{:S(2)}) collective-permute-start(bf16[160,256]{1,0:T(8,128)(2,1)S(1)} %get-tuple-element.57), channel_id=1, source_target_pairs={{0,2},{1,3},{2,0},{3,1},{4,6},{5,7},{6,4},{7,5},{8,10},{9,11},{10,... | collective-permute-start | bytes 245768 | tf_op jit(solution)/shard_map/ppermute | solution.py:46
  25.6 1.3 %collective-permute-start.8 = (bf16[160,256]{1,0:T(8,128)(2,1)S(1)}, bf16[160,256]{1,0:T(8,128)(2,1)S(1)}, u32[]{:S(2)}, u32[]{:S(2)}) collective-permute-start(bf16[160,256]{1,0:T(8,128)(2,1)S(1)} %get-tuple-element.56), channel_id=1, source_target_pairs={{0,1},{1,2},{2,3},{3,0},{4,5},{5,6},{6,7},{7,4},{8,9},{9,10},{10,1... | collective-permute-start | bytes 245768 | tf_op jit(solution)/shard_map/ppermute | solution.py:46
  26.9 2.5 %collective-permute-start.11 = (bf16[160,256]{1,0:T(8,128)(2,1)S(1)}, bf16[160,256]{1,0:T(8,128)(2,1)S(1)}, u32[]{:S(2)}, u32[]{:S(2)}) collective-permute-start(bf16[160,256]{1,0:T(8,128)(2,1)S(1)} %get-tuple-element.60), channel_id=1, source_target_pairs={{0,3},{1,0},{2,1},{3,2},{4,7},{5,4},{6,5},{7,6},{8,11},{9,8},{10,9... | collective-permute-start | bytes 245768 | tf_op jit(solution)/shard_map/ppermute | solution.py:46
  29.5 0.0 collective-permute-done.10.refs_2_
  29.5 3.5 %collective-permute-done.9.refs_0_ = bf16[160,256]{1,0:T(8,128)(2,1)S(1)} collective-permute-done((bf16[160,256]{1,0:T(8,128)(2,1)S(1)}, bf16[160,256]{1,0:T(8,128)(2,1)S(1)}, u32[]{:S(2)}, u32[]{:S(2)}) %collective-permute-start.9) | collective-permute-done | bytes 81952 | tf_op jit(solution)/shard_map/ppermute | solution.py:46
  33.0 0.0 copy-start.2
  33.0 0.0 collective-permute-done.8.refs_1_
  33.0 0.1 collective-permute-done.11.refs_3_
  33.2 0.0 collective-permute-done.12.refs_1_
  33.2 0.1 collective-permute-start.13
  33.3 1.3 %collective-permute-start.15 = (bf16[640,256]{1,0:T(8,128)(2,1)S(1)}, bf16[640,256]{1,0:T(8,128)(2,1)S(1)}, u32[]{:S(2)}, u32[]{:S(2)}) collective-permute-start(bf16[640,256]{1,0:T(8,128)(2,1)S(1)} %get-tuple-element.63.refs_1_), channel_id=1, source_target_pairs={{0,1},{1,3},{2,0},{3,2},{4,5},{5,7},{6,4},{7,6},{8,9},{9,11},{10,8... | collective-permute-start | bytes 983048 | tf_op jit(solution)/shard_map/ppermute | solution.py:100
  34.6 1.7 %collective-permute-start.14 = (bf16[640,256]{1,0:T(8,128)(2,1)S(1)}, bf16[640,256]{1,0:T(8,128)(2,1)S(1)}, u32[]{:S(2)}, u32[]{:S(2)}) collective-permute-start(bf16[640,256]{1,0:T(8,128)(2,1)S(1)} %get-tuple-element.64.refs_2_), channel_id=1, source_target_pairs={{0,2},{1,0},{2,3},{3,1},{4,6},{5,4},{6,7},{7,5},{8,10},{9,8},{10,1... | collective-permute-start | bytes 983048 | tf_op jit(solution)/shard_map/ppermute | solution.py:100
  36.3 2.4 %collective-permute-start.18 = (bf16[640,256]{1,0:T(8,128)(2,1)S(1)}, bf16[640,256]{1,0:T(8,128)(2,1)S(1)}, u32[]{:S(2)}, u32[]{:S(2)}) collective-permute-start(bf16[640,256]{1,0:T(8,128)(2,1)S(1)} %get-tuple-element.65.refs_3_), channel_id=1, source_target_pairs={{0,12},{4,8},{8,4},{12,0},{1,13},{5,9},{9,5},{13,1},{2,14},{6,10},... | collective-permute-start | bytes 983048 | tf_op jit(solution)/shard_map/ppermute | solution.py:41
  38.8 0.5 collective-permute-start.17
  39.3 0.0 collective-permute-done.13.refs_1_
  39.3 0.5 collective-permute-start.16
  39.8 0.0 copy-done.2
  39.8 0.0 copy-done.3
  39.8 0.0 copy-done.5
  39.8 0.0 copy-done.7
  39.8 1.5 %shard_map.66.refs_1_ = bf16[5,10,128,128]{3,2,1,0:T(8,128)(2,1)S(1)} custom-call(s32[2,4,6]{2,1,0:T(4,128)S(1)} %bitcast.22, s32[5,1,10]{2,1,0:T(1,128)S(1)} %bitcast.24, bf16[5,10,128,128]{3,2,1,0:T(8,128)(2,1)S(1)} %bitcast.20, bf16[6,6,128,128]{3,2,1,0:T(8,128)(2,1)S(1)} %bitcast.18, bf16[6,6,128,128]{3,2,1,0:T(8,128)(2,1)S(1)} %collective-permute-done.received_ref, ...), custom_call_target="tpu_custom_call" | custom-call | bytes 6291456 | tf_op jit(solution)/shard_map/pallas_call | solution.py:475
  41.3 0.8 %shard_map.64.inverse_ref.refs_2_ = bf16[1024,1024]{1,0:T(8,128)(2,1)S(1)} custom-call(bf16[1280,256]{1,0:T(8,128)(2,1)S(1)} %get-tuple-element.62.refs_0_, bf16[1280,256]{1,0:T(8,128)(2,1)S(1)} %collective-permute-done.13.refs_1_), custom_call_target="tpu_custom_call" | custom-call | bytes 4194304 | tf_op jit(solution)/shard_map/pallas_call | solution.py:461
  42.1 2.3 %collective-permute-done.15.refs_4_ = bf16[640,256]{1,0:T(8,128)(2,1)S(1)} collective-permute-done((bf16[640,256]{1,0:T(8,128)(2,1)S(1)}, bf16[640,256]{1,0:T(8,128)(2,1)S(1)}, u32[]{:S(2)}, u32[]{:S(2)}) %collective-permute-start.15) | collective-permute-done | bytes 327712 | tf_op jit(solution)/shard_map/ppermute | solution.py:100
  44.4 6.9 %collective-permute-done.14.refs_3_ = bf16[640,256]{1,0:T(8,128)(2,1)S(1)} collective-permute-done((bf16[640,256]{1,0:T(8,128)(2,1)S(1)}, bf16[640,256]{1,0:T(8,128)(2,1)S(1)}, u32[]{:S(2)}, u32[]{:S(2)}) %collective-permute-start.14) | collective-permute-done | bytes 327712 | tf_op jit(solution)/shard_map/ppermute | solution.py:100
  51.4 1.4 %shard_map.65.refs_0_ = bf16[640,1024]{1,0:T(8,128)(2,1)S(1)} custom-call(bf16[1024,1024]{1,0:T(8,128)(2,1)S(1)} %shard_map.64.inverse_ref.refs_2_, bf16[640,256]{1,0:T(8,128)(2,1)S(1)} %get-tuple-element.45.refs_0_.piece_ref, bf16[640,256]{1,0:T(8,128)(2,1)S(1)} %get-tuple-element.63.refs_1_, bf16[640,256]{1,0:T(8,128)(2,1)S(1)} %get-tuple-element.64.refs_2_, ...), custom_call_target="tpu_custom_call" | custom-call | flops 1006632960 | bytes 524288 | tf_op jit(solution)/shard_map/pallas_call | solution.py:484
  52.8 0.0 collective-permute-done.18.refs_6_
  52.8 0.9 %collective-permute-done.17.refs_5_ = bf16[640,256]{1,0:T(8,128)(2,1)S(1)} collective-permute-done((bf16[640,256]{1,0:T(8,128)(2,1)S(1)}, bf16[640,256]{1,0:T(8,128)(2,1)S(1)}, u32[]{:S(2)}, u32[]{:S(2)}) %collective-permute-start.17) | collective-permute-done | bytes 327712 | tf_op jit(solution)/shard_map/ppermute | solution.py:41
  53.7 0.1 collective-permute-done.16.refs_4_
  53.8 1.4 %shard_map.68 = (bf16[640,512]{1,0:T(8,128)(2,1)S(1)}, bf16[640,512]{1,0:T(8,128)(2,1)S(1)}) custom-call(bf16[1024,1024]{1,0:T(8,128)(2,1)S(1)} %get-tuple-element.68.inverse_ref, bf16[640,256]{1,0:T(8,128)(2,1)S(1)} %get-tuple-element.69.refs_0_, bf16[640,256]{1,0:T(8,128)(2,1)S(1)} %get-tuple-element.70.refs_1_, ...), custom_call_target="tpu_custom_call" | custom-call | flops 1006632960 | bytes 524288 | tf_op jit(solution)/shard_map/pallas_call | solution.py:492
  55.3 0.1 collective-permute-start.19
  55.4 0.5 collective-permute-start.20
  55.9 2.0 %shard_map.69.refs_2_ = bf16[5,5,2,128,128]{4,3,2,1,0:T(8,128)(2,1)} custom-call(bf16[640,1024]{1,0:T(8,128)(2,1)S(1)} %get-tuple-element.66.rows_ref, bf16[5,5,2,128,128]{4,3,2,1,0:T(8,128)(2,1)S(1)} %bitcast.14, bf16[640,512]{1,0:T(8,128)(2,1)S(1)} %get-tuple-element.73.refs_0_, bf16[640,512]{1,0:T(8,128)(2,1)S(1)} %get-tuple-element.74.refs_1_), custom_call_target="tpu_custom_call" | custom-call | flops 838860800 | bytes 524288 | tf_op jit(solution)/shard_map/pallas_call | solution.py:507
  57.9 0.0 collective-permute-done.19.refs_0_
  57.9 0.5 collective-permute-done.20.refs_1_
  58.4 2.0 %shard_map.70 = bf16[5,5,2,128,128]{4,3,2,1,0:T(8,128)(2,1)} custom-call(bf16[640,1024]{1,0:T(8,128)(2,1)S(1)} %get-tuple-element.66.rows_ref, bf16[5,5,2,128,128]{4,3,2,1,0:T(8,128)(2,1)S(1)} %bitcast.15, bf16[640,512]{1,0:T(8,128)(2,1)S(1)} %collective-permute-done.19.refs_0_, ...), custom_call_target="tpu_custom_call", output_to_operand_aliasing={{}: (4, {})} | custom-call | flops 838860800 | bytes 524288 | tf_op jit(solution)/shard_map/pallas_call | solution.py:510
  (12 shorter events, 0.1 us)
Async XLA Ops:
  0.0 1.0 %copy-start = (bf16[256,1024]{1,0:T(8,128)(2,1)S(1)}, bf16[256,1024]{1,0:T(8,128)(2,1)}, u32[]{:S(2)}) copy-start(bf16[256,1024]{1,0:T(8,128)(2,1)} %param.9) | copy-start | bytes 1572868
  0.0 8.1 %collective-permute-start = (bf16[6,6,128,128]{3,2,1,0:T(8,128)(2,1)}, bf16[6,6,128,128]{3,2,1,0:T(8,128)(2,1)S(1)}, u32[]{:S(2)}, u32[]{:S(2)}) collective-permute-start(bf16[6,6,128,128]{3,2,1,0:T(8,128)(2,1)} %bitcast.16), channel_id=1, source_target_pairs={{0,16},{16,0},{1,17},{17,1},{2,18},{18,2},{3,19},{19,3},{4,20},{20... | collective-permute-start | bytes 3538952 | tf_op jit(solution)/shard_map/ppermute | solution.py:41
  1.0 10.7 %collective-permute-start.3 = (bf16[32,1024]{1,0:T(8,128)(2,1)S(1)}, bf16[32,1024]{1,0:T(8,128)(2,1)S(1)}, u32[]{:S(2)}, u32[]{:S(2)}) collective-permute-start(bf16[32,1024]{1,0:T(8,128)(2,1)S(1)} %constant_dynamic-slice_fusion.refs_1_), channel_id=1, source_target_pairs={{0,2},{1,3},{2,0},{3,1},{4,6},{5,7},{6,4},{7,5},{8,10},{9,11},{10,... | collective-permute-start | bytes 196616 | tf_op jit(solution)/shard_map/ppermute | solution.py:46
  5.1 6.7 %collective-permute-start.2 = (bf16[32,1024]{1,0:T(8,128)(2,1)S(1)}, bf16[32,1024]{1,0:T(8,128)(2,1)S(1)}, u32[]{:S(2)}, u32[]{:S(2)}) collective-permute-start(bf16[32,1024]{1,0:T(8,128)(2,1)S(1)} %constant_dynamic-slice_fusion.refs_1_), channel_id=1, source_target_pairs={{0,3},{1,0},{2,1},{3,2},{4,7},{5,4},{6,5},{7,6},{8,11},{9,8},{10,9... | collective-permute-start | bytes 196616 | tf_op jit(solution)/shard_map/ppermute | solution.py:46
  6.4 6.1 %collective-permute-start.1 = (bf16[32,1024]{1,0:T(8,128)(2,1)S(1)}, bf16[32,1024]{1,0:T(8,128)(2,1)S(1)}, u32[]{:S(2)}, u32[]{:S(2)}) collective-permute-start(bf16[32,1024]{1,0:T(8,128)(2,1)S(1)} %constant_dynamic-slice_fusion.refs_1_), channel_id=1, source_target_pairs={{0,1},{1,2},{2,3},{3,0},{4,5},{5,6},{6,7},{7,4},{8,9},{9,10},{10,1... | collective-permute-start | bytes 196616 | tf_op jit(solution)/shard_map/ppermute | solution.py:46
  8.1 1.3 %copy-start.1 = (bf16[1,6,1,128,6,1,128]{6,3,5,4,2,1,0:T(8,128)(2,1)S(1)}, bf16[1,6,1,128,6,1,128]{6,3,5,4,2,1,0:T(8,128)(2,1)}, u32[]{:S(2)}) copy-start(bf16[1,6,1,128,6,1,128]{6,3,5,4,2,1,0:T(8,128)(2,1)} %param.7) | copy-start | bytes 3538948
  9.4 0.7 %copy-start.4 = (s32[2,6,4]{1,2,0:T(4,128)S(1)}, s32[2,6,4]{1,2,0:T(4,128)}, u32[]{:S(2)}) copy-start(s32[2,6,4]{1,2,0:T(4,128)} %param.8) | copy-start | bytes 580
  10.1 0.7 %copy-start.6 = (s32[5,1,1,10,1]{3,4,2,1,0:T(1,128)S(1)}, s32[5,1,1,10,1]{3,4,2,1,0:T(1,128)}, u32[]{:S(2)}) copy-start(s32[5,1,1,10,1]{3,4,2,1,0:T(1,128)} %param.6) | copy-start | bytes 604
  12.6 10.3 %collective-permute-start.4 = (bf16[640,256]{1,0:T(8,128)(2,1)S(1)}, bf16[640,256]{1,0:T(8,128)(2,1)S(1)}, u32[]{:S(2)}, u32[]{:S(2)}) collective-permute-start(bf16[640,256]{1,0:T(8,128)(2,1)S(1)} %get-tuple-element.45.refs_0_.piece_ref), channel_id=1, source_target_pairs={{0,1},{1,0},{2,3},{3,2},{4,5},{5,4},{6,7},{7,6},{8,9},{9,8},{10,11... | collective-permute-start | bytes 983048 | tf_op jit(solution)/shard_map/ppermute | solution.py:100
  13.5 9.3 %collective-permute-start.5 = (bf16[480,256]{1,0:T(8,128)(2,1)S(1)}, bf16[480,256]{1,0:T(8,128)(2,1)S(1)}, u32[]{:S(2)}, u32[]{:S(2)}) collective-permute-start(bf16[480,256]{1,0:T(8,128)(2,1)S(1)} %get-tuple-element.47.refs_4_), channel_id=1, source_target_pairs={{0,4},{4,0},{8,12},{12,8},{1,5},{5,1},{9,13},{13,9},{2,6},{6,2},{1... | collective-permute-start | bytes 737288 | tf_op jit(solution)/shard_map/ppermute | solution.py:41
  15.0 5.2 %collective-permute-start.6 = (bf16[160,256]{1,0:T(8,128)(2,1)S(1)}, bf16[160,256]{1,0:T(8,128)(2,1)S(1)}, u32[]{:S(2)}, u32[]{:S(2)}) collective-permute-start(bf16[160,256]{1,0:T(8,128)(2,1)S(1)} %get-tuple-element.48), channel_id=1, source_target_pairs={{0,8},{4,12},{8,0},{12,4},{1,9},{5,13},{9,1},{13,5},{2,10},{6,14},... | collective-permute-start | bytes 245768 | tf_op jit(solution)/shard_map/ppermute | solution.py:41
  16.5 6.3 %collective-permute-start.7 = (bf16[160,256]{1,0:T(8,128)(2,1)S(1)}, bf16[160,256]{1,0:T(8,128)(2,1)S(1)}, u32[]{:S(2)}, u32[]{:S(2)}) collective-permute-start(bf16[160,256]{1,0:T(8,128)(2,1)S(1)} %get-tuple-element.49), channel_id=1, source_target_pairs={{0,12},{4,8},{8,4},{12,0},{1,13},{5,9},{9,5},{13,1},{2,14},{6,10},... | collective-permute-start | bytes 245768 | tf_op jit(solution)/shard_map/ppermute | solution.py:41
  17.0 12.5 %collective-permute-start.10 = (bf16[640,256]{1,0:T(8,128)(2,1)S(1)}, bf16[640,256]{1,0:T(8,128)(2,1)S(1)}, u32[]{:S(2)}, u32[]{:S(2)}) collective-permute-start(bf16[640,256]{1,0:T(8,128)(2,1)S(1)} %get-tuple-element.45.refs_0_.piece_ref), channel_id=1, source_target_pairs={{0,0},{1,2},{2,1},{3,3},{4,4},{5,6},{6,5},{7,7},{8,8},{9,10},{10,9... | collective-permute-start | bytes 983048 | tf_op jit(solution)/shard_map/ppermute | solution.py:100
  22.9 10.2 %collective-permute-start.12 = (bf16[640,256]{1,0:T(8,128)(2,1)S(1)}, bf16[640,256]{1,0:T(8,128)(2,1)S(1)}, u32[]{:S(2)}, u32[]{:S(2)}) collective-permute-start(bf16[640,256]{1,0:T(8,128)(2,1)S(1)} %get-tuple-element.61.refs_0_), channel_id=1, source_target_pairs={{0,8},{4,12},{8,0},{12,4},{1,9},{5,13},{9,1},{13,5},{2,10},{6,14},... | collective-permute-start | bytes 983048 | tf_op jit(solution)/shard_map/ppermute | solution.py:41
  23.5 9.5 %collective-permute-start.9 = (bf16[160,256]{1,0:T(8,128)(2,1)S(1)}, bf16[160,256]{1,0:T(8,128)(2,1)S(1)}, u32[]{:S(2)}, u32[]{:S(2)}) collective-permute-start(bf16[160,256]{1,0:T(8,128)(2,1)S(1)} %get-tuple-element.57), channel_id=1, source_target_pairs={{0,2},{1,3},{2,0},{3,1},{4,6},{5,7},{6,4},{7,5},{8,10},{9,11},{10,... | collective-permute-start | bytes 245768 | tf_op jit(solution)/shard_map/ppermute | solution.py:46
  25.6 7.3 %collective-permute-start.8 = (bf16[160,256]{1,0:T(8,128)(2,1)S(1)}, bf16[160,256]{1,0:T(8,128)(2,1)S(1)}, u32[]{:S(2)}, u32[]{:S(2)}) collective-permute-start(bf16[160,256]{1,0:T(8,128)(2,1)S(1)} %get-tuple-element.56), channel_id=1, source_target_pairs={{0,1},{1,2},{2,3},{3,0},{4,5},{5,6},{6,7},{7,4},{8,9},{9,10},{10,1... | collective-permute-start | bytes 245768 | tf_op jit(solution)/shard_map/ppermute | solution.py:46
  26.9 6.2 %collective-permute-start.11 = (bf16[160,256]{1,0:T(8,128)(2,1)S(1)}, bf16[160,256]{1,0:T(8,128)(2,1)S(1)}, u32[]{:S(2)}, u32[]{:S(2)}) collective-permute-start(bf16[160,256]{1,0:T(8,128)(2,1)S(1)} %get-tuple-element.60), channel_id=1, source_target_pairs={{0,3},{1,0},{2,1},{3,2},{4,7},{5,4},{6,5},{7,6},{8,11},{9,8},{10,9... | collective-permute-start | bytes 245768 | tf_op jit(solution)/shard_map/ppermute | solution.py:46
  33.0 6.8 %copy-start.2 = (bf16[1,6,1,128,6,1,128]{6,3,5,4,2,1,0:T(8,128)(2,1)S(1)}, bf16[1,6,1,128,6,1,128]{6,3,5,4,2,1,0:T(8,128)(2,1)}, u32[]{:S(2)}) copy-start(bf16[1,6,1,128,6,1,128]{6,3,5,4,2,1,0:T(8,128)(2,1)} %param.7) | copy-start | bytes 3538948
  33.0 6.8 %copy-start.3 = (bf16[5,1,1,128,10,1,128]{6,3,5,4,2,1,0:T(8,128)(2,1)S(1)}, bf16[5,1,1,128,10,1,128]{6,3,5,4,2,1,0:T(8,128)(2,1)}, u32[]{:S(2)}) copy-start(bf16[5,1,1,128,10,1,128]{6,3,5,4,2,1,0:T(8,128)(2,1)} %param.5) | copy-start | bytes 4915204
  33.0 6.8 %copy-start.5 = (s32[2,6,4]{1,2,0:T(4,128)S(1)}, s32[2,6,4]{1,2,0:T(4,128)}, u32[]{:S(2)}) copy-start(s32[2,6,4]{1,2,0:T(4,128)} %param.8) | copy-start | bytes 580
  33.0 6.8 %copy-start.7 = (s32[5,1,1,10,1]{3,4,2,1,0:T(1,128)S(1)}, s32[5,1,1,10,1]{3,4,2,1,0:T(1,128)}, u32[]{:S(2)}) copy-start(s32[5,1,1,10,1]{3,4,2,1,0:T(1,128)} %param.6) | copy-start | bytes 604
  33.2 6.0 %collective-permute-start.13 = (bf16[1280,256]{1,0:T(8,128)(2,1)S(1)}, bf16[1280,256]{1,0:T(8,128)(2,1)S(1)}, u32[]{:S(2)}, u32[]{:S(2)}) collective-permute-start(bf16[1280,256]{1,0:T(8,128)(2,1)S(1)} %get-tuple-element.62.refs_0_), channel_id=1, source_target_pairs={{0,16},{16,0},{1,17},{17,1},{2,18},{18,2},{3,19},{19,3},{4,20},{20... | collective-permute-start | bytes 1966088 | tf_op jit(solution)/shard_map/ppermute | solution.py:41
  33.3 11.1 %collective-permute-start.15 = (bf16[640,256]{1,0:T(8,128)(2,1)S(1)}, bf16[640,256]{1,0:T(8,128)(2,1)S(1)}, u32[]{:S(2)}, u32[]{:S(2)}) collective-permute-start(bf16[640,256]{1,0:T(8,128)(2,1)S(1)} %get-tuple-element.63.refs_1_), channel_id=1, source_target_pairs={{0,1},{1,3},{2,0},{3,2},{4,5},{5,7},{6,4},{7,6},{8,9},{9,11},{10,8... | collective-permute-start | bytes 983048 | tf_op jit(solution)/shard_map/ppermute | solution.py:100
  34.6 16.8 %collective-permute-start.14 = (bf16[640,256]{1,0:T(8,128)(2,1)S(1)}, bf16[640,256]{1,0:T(8,128)(2,1)S(1)}, u32[]{:S(2)}, u32[]{:S(2)}) collective-permute-start(bf16[640,256]{1,0:T(8,128)(2,1)S(1)} %get-tuple-element.64.refs_2_), channel_id=1, source_target_pairs={{0,2},{1,0},{2,3},{3,1},{4,6},{5,4},{6,7},{7,5},{8,10},{9,8},{10,1... | collective-permute-start | bytes 983048 | tf_op jit(solution)/shard_map/ppermute | solution.py:100
  36.3 16.5 %collective-permute-start.18 = (bf16[640,256]{1,0:T(8,128)(2,1)S(1)}, bf16[640,256]{1,0:T(8,128)(2,1)S(1)}, u32[]{:S(2)}, u32[]{:S(2)}) collective-permute-start(bf16[640,256]{1,0:T(8,128)(2,1)S(1)} %get-tuple-element.65.refs_3_), channel_id=1, source_target_pairs={{0,12},{4,8},{8,4},{12,0},{1,13},{5,9},{9,5},{13,1},{2,14},{6,10},... | collective-permute-start | bytes 983048 | tf_op jit(solution)/shard_map/ppermute | solution.py:41
  38.8 15.0 %collective-permute-start.17 = (bf16[640,256]{1,0:T(8,128)(2,1)S(1)}, bf16[640,256]{1,0:T(8,128)(2,1)S(1)}, u32[]{:S(2)}, u32[]{:S(2)}) collective-permute-start(bf16[640,256]{1,0:T(8,128)(2,1)S(1)} %get-tuple-element.65.refs_3_), channel_id=1, source_target_pairs={{0,8},{4,12},{8,0},{12,4},{1,9},{5,13},{9,1},{13,5},{2,10},{6,14},... | collective-permute-start | bytes 983048 | tf_op jit(solution)/shard_map/ppermute | solution.py:41
  39.3 14.6 %collective-permute-start.16 = (bf16[640,256]{1,0:T(8,128)(2,1)S(1)}, bf16[640,256]{1,0:T(8,128)(2,1)S(1)}, u32[]{:S(2)}, u32[]{:S(2)}) collective-permute-start(bf16[640,256]{1,0:T(8,128)(2,1)S(1)} %get-tuple-element.65.refs_3_), channel_id=1, source_target_pairs={{0,4},{4,0},{8,12},{12,8},{1,5},{5,1},{9,13},{13,9},{2,6},{6,2},{1... | collective-permute-start | bytes 983048 | tf_op jit(solution)/shard_map/ppermute | solution.py:41
  55.3 2.6 %collective-permute-start.19 = (bf16[640,512]{1,0:T(8,128)(2,1)S(1)}, bf16[640,512]{1,0:T(8,128)(2,1)S(1)}, u32[]{:S(2)}, u32[]{:S(2)}) collective-permute-start(bf16[640,512]{1,0:T(8,128)(2,1)S(1)} %get-tuple-element.73.refs_0_), channel_id=1, source_target_pairs={{0,16},{16,0},{1,17},{17,1},{2,18},{18,2},{3,19},{19,3},{4,20},{20... | collective-permute-start | bytes 1966088 | tf_op jit(solution)/shard_map/ppermute | solution.py:41
  55.4 3.0 %collective-permute-start.20 = (bf16[640,512]{1,0:T(8,128)(2,1)S(1)}, bf16[640,512]{1,0:T(8,128)(2,1)S(1)}, u32[]{:S(2)}, u32[]{:S(2)}) collective-permute-start(bf16[640,512]{1,0:T(8,128)(2,1)S(1)} %get-tuple-element.74.refs_1_), channel_id=1, source_target_pairs={{0,16},{16,0},{1,17},{17,1},{2,18},{18,2},{3,19},{19,3},{4,20},{20... | collective-permute-start | bytes 1966088 | tf_op jit(solution)/shard_map/ppermute | solution.py:41
